TPU v7x, 128 devices: a whole 4x4x4 slice. The times are simulated.
128 devices in a mesh: dp: 2 (over y_hi), seq: 8 (over y_lo, x), tensor: 8 (over z, core).
Axes of the slice: x: 4, y: 4 (y_hi: 2, y_lo: 2; y = y_hi * 2 + y_lo), z: 4, core: 2. Of those that a mesh axis runs over, the one named last changes fastest.
Arguments:
- tokens: bfloat16 [16384, 2048], P(('dp', 'seq')), parts along dimension 0, may hold values from -6 to 6
- doc_ids: int32 [16384], P('dp'), parts along dimension 0, may hold values from 0 to 3, never falling along the last dimension, each value on 1 to 4096 neighbouring positions
- mlp_gain: bfloat16 [2048], replicated, may hold values from 0.099609375 to 1.8984375
- gate_weight: bfloat16 [2048, 8192], P(None, 'tensor'), may hold values from -0.125 to 0.125
- up_weight: bfloat16 [2048, 8192], P(None, 'tensor'), may hold values from -0.125 to 0.125
- down_weight: bfloat16 [8192, 2048], P('tensor'), may hold values from -0.0625 to 0.0625
- attn_gain: bfloat16 [2048], replicated, may hold values from 0.099609375 to 1.8984375
- query_weight: bfloat16 [2048, 2048], P(None, 'tensor'), may hold values from -8 to 8
- key_weight: bfloat16 [2048, 2048], P(None, 'tensor'), may hold values from -1 to 1
- value_weight: bfloat16 [2048, 2048], P(None, 'tensor'), may hold values from -0.125 to 0.125
- out_weight: bfloat16 [2048, 2048], P('tensor'), may hold values from -0.125 to 0.125
Outputs:
- layer_out: bfloat16 [16384, 2048], P(('dp', 'seq', 'tensor')), parts along dimension 0
There are 2 independent parts, one for each index of `dp`. A program takes and returns all parts, laid end to end along the dimension named above; an argument that names none is the same for every part. Nothing has to cross between parts.
Inputs may be any that keep to these rules, and one draw needn't show every extreme that they name: doc_ids never falls along the positions; each document covers 1 to 4096 positions, one of them exactly 4096.
All inputs are finite; a program needn't handle non-finite values.
Results may differ from a plain program's by a relative error of at most 0.01325.
Values may be sent and summed in bfloat16 or wider, within the bound.
A program may use at most 128 MiB of HBM per device.

v0:
```python
import jax
import jax.numpy as jnp
from jax import lax
from jax.sharding import PartitionSpec as P

HEAD_DIM = 128


EPSILON = 1e-05
ROPE_BASE = 500000.0
NEGATIVE = -1e30


def rms_scale(values, gain):
    mean_square = jnp.mean(values * values, axis=-1, keepdims=True)
    return values * lax.rsqrt(mean_square + EPSILON) * gain.astype(jnp.float32)


def row_positions(seq_group, local_rows, rows_dev, groups, splits):
    slice_rows = rows_dev // (groups * splits)
    half_rows = rows_dev // (2 * groups)
    tensor_part = local_rows // (groups * slice_rows)
    source_group = local_rows // slice_rows % groups
    within = local_rows % slice_rows
    offset = tensor_part * slice_rows + within
    which_block = jnp.where(offset < half_rows, seq_group, 2 * groups - 1 - seq_group)
    return source_group * rows_dev + which_block * half_rows + offset % half_rows


def rotate(values, positions, head_dim):
    row_count = values.shape[0]
    shaped = values.reshape(row_count, -1, head_dim)
    half_dim = head_dim // 2
    frequency = ROPE_BASE ** (-(jnp.arange(half_dim, dtype=jnp.float32) / half_dim))
    angles = positions.astype(jnp.float32)[:, None] * frequency[None, :]
    cosine = jnp.cos(angles)[:, None, :]
    sine_part = jnp.sin(angles)[:, None, :]
    front_half = shaped[..., :half_dim]
    back_half = shaped[..., half_dim:]
    turned = jnp.concatenate(
        [front_half * cosine - back_half * sine_part, back_half * cosine + front_half * sine_part],
        axis=-1,
    )
    return turned.reshape(row_count, -1)


def pair_blocks(values, groups, half_rows):
    blocks = values.reshape(2 * groups, half_rows, values.shape[-1])
    paired = jnp.stack([blocks[:groups], blocks[groups:][::-1]], axis=1)
    return paired.reshape(groups, 2 * half_rows, values.shape[-1])


def body(
    tokens,
    doc_ids,
    mlp_gain,
    gate_weight,
    up_weight,
    down_weight,
    attn_gain,
    query_weight,
    key_weight,
    value_weight,
    out_weight,
):
    groups = lax.axis_size("seq")
    splits = lax.axis_size("tensor")
    rows_dev, width = tokens.shape
    half_rows = rows_dev // (2 * groups)
    slice_rows = rows_dev // (groups * splits)
    seq_group = lax.axis_index("seq")
    tensor_part = lax.axis_index("tensor")
    mlp_in = rms_scale(tokens.astype(jnp.float32), mlp_gain).astype(jnp.bfloat16)
    gate = jnp.dot(mlp_in, gate_weight, preferred_element_type=jnp.float32)
    up_part = jnp.dot(mlp_in, up_weight, preferred_element_type=jnp.float32)
    hidden = (jax.nn.silu(gate) * up_part).astype(jnp.bfloat16)
    partial_value = jnp.dot(hidden, down_weight, preferred_element_type=jnp.float32)
    own_share = jnp.where(tensor_part == 0, 1.0, 0.0).astype(jnp.float32)
    term = partial_value + own_share * tokens.astype(jnp.float32)
    outgoing = pair_blocks(term, groups, half_rows).reshape(groups * splits, slice_rows, width)
    arrived = lax.all_to_all(outgoing, ("seq", "tensor"), split_axis=0, concat_axis=0, tiled=True)
    stream = (
        jnp.sum(arrived.reshape(groups, splits, slice_rows, width), axis=1)
        .reshape(-1, width)
        .astype(jnp.bfloat16)
    )
    attn_in = rms_scale(stream.astype(jnp.float32), attn_gain).astype(jnp.bfloat16)
    head_width = query_weight.shape[1]
    heads_dev = head_width // HEAD_DIM
    joined_weight = jnp.concatenate([query_weight, key_weight, value_weight], axis=1)
    shard_piece = lax.all_gather(attn_in, "tensor", axis=0, tiled=True)
    local_rows = jnp.arange(shard_piece.shape[0], dtype=jnp.int32)
    positions = row_positions(seq_group, local_rows, rows_dev, groups, splits)
    projected = jnp.dot(shard_piece, joined_weight, preferred_element_type=jnp.float32)
    query_turned = rotate(projected[:, :head_width], positions, HEAD_DIM)
    key_turned = rotate(projected[:, head_width : 2 * head_width], positions, HEAD_DIM)
    projected_rows = jnp.concatenate(
        [query_turned, key_turned, projected[:, 2 * head_width :]], axis=1
    ).astype(jnp.bfloat16)
    queries = projected_rows[:, :head_width].reshape(rows_dev, heads_dev, HEAD_DIM)
    key_values = projected_rows[:, head_width:]
    query_pos = row_positions(
        seq_group, jnp.arange(rows_dev, dtype=jnp.int32), rows_dev, groups, splits
    )
    query_docs = doc_ids[query_pos]
    score_scale = HEAD_DIM ** (-0.5)
    start_state = (
        jnp.full((heads_dev, rows_dev), NEGATIVE, jnp.float32),
        jnp.zeros((heads_dev, rows_dev), jnp.float32),
        jnp.zeros((heads_dev, rows_dev, HEAD_DIM), jnp.float32),
    )
    shard_piece = lax.all_gather(key_values, "seq", axis=0, tiled=True)
    piece_rows = shard_piece.shape[0]
    block_rows = min(piece_rows, rows_dev)

    def one_step(state_then, step_index):
        running_max, running_sum, weighted = state_then
        block_kv = lax.dynamic_slice_in_dim(shard_piece, step_index * block_rows, block_rows, 0)
        key_block = block_kv[:, :head_width].reshape(block_rows, heads_dev, HEAD_DIM)
        value_block = block_kv[:, head_width:].reshape(block_rows, heads_dev, HEAD_DIM)
        global_rows = step_index * block_rows + jnp.arange(block_rows, dtype=jnp.int32)
        key_pos = row_positions(
            global_rows // rows_dev, global_rows % rows_dev, rows_dev, groups, splits
        )
        allowed = (key_pos[None, :] <= query_pos[:, None]) & (
            doc_ids[key_pos][None, :] == query_docs[:, None]
        )
        scores = (
            jnp.einsum("qhd,khd->hqk", queries, key_block, preferred_element_type=jnp.float32)
            * score_scale
        )
        scores = jnp.where(allowed[None], scores, NEGATIVE)
        new_max = jnp.maximum(running_max, jnp.max(scores, axis=2))
        weights = jnp.where(allowed[None], jnp.exp(scores - new_max[:, :, None]), 0.0)
        rescale = jnp.exp(running_max - new_max)
        running_sum = running_sum * rescale + jnp.sum(weights, axis=2)
        weighted = weighted * rescale[:, :, None] + jnp.einsum(
            "hqk,khd->hqd",
            weights.astype(jnp.bfloat16),
            value_block,
            preferred_element_type=jnp.float32,
        )
        return ((new_max, running_sum, weighted), None)

    finished = lax.scan(
        one_step, start_state, jnp.arange(piece_rows // block_rows, dtype=jnp.int32)
    )
    running_max, running_sum, weighted = finished[0]
    context = (
        (weighted / running_sum[:, :, None])
        .transpose(1, 0, 2)
        .reshape(rows_dev, head_width)
        .astype(jnp.bfloat16)
    )
    summed_out = lax.psum_scatter(
        jnp.dot(context, out_weight, preferred_element_type=jnp.float32).astype(jnp.bfloat16),
        "tensor",
        scatter_dimension=0,
        tiled=True,
    ).astype(jnp.float32)
    return (stream.astype(jnp.float32) + summed_out).astype(jnp.bfloat16)


def solution(mesh):
    in_specs = (
        P(("dp", "seq"), None),
        P("dp"),
        P(),
        P(None, "tensor"),
        P(None, "tensor"),
        P("tensor", None),
        P(),
        P(None, "tensor"),
        P(None, "tensor"),
        P(None, "tensor"),
        P("tensor", None),
    )
    out_specs = P(("dp", "seq", "tensor"), None)
    return jax.shard_map(body, mesh=mesh, in_specs=in_specs, out_specs=out_specs, check_vma=False)
```

profile of v0, /device:TPU:0, one launch (start us, length us, event | category | flops | bytes accessed | tf_op | source)
XLA Modules:
  0.0 529.0 jit_solution(17205158675089155934)
XLA Ops:
  6.5 3.2 fusion.56
  9.8 10.0 %fusion.67 = f32[1024,1024]{1,0:T(8,128)} fusion(bf16[2048,1024]{1,0:T(8,128)(2,1)} %param.16, bf16[1024,2048]{1,0:T(8,128)(2,1)} %param.13, f32[2048]{0:T(1024)S(1)} %convert_element_type.69, f32[1024]{0:T(1024)S(1)} %add_rsqrt_fusion.1), kind=kOutput, calls=%fused_computation.139 | convolution fusion | flops 4303355904 | bytes 12595200 | tf_op jit(solution)/shard_map/dot_general | solution.py:74
  19.7 17.2 %fusion.59 = f32[1024,2048]{1,0:T(8,128)} fusion(bf16[1024,2048]{1,0:T(8,128)(2,1)} %param.13, f32[]{:T(128)S(6)} %select_n.370, bf16[1024,2048]{1,0:T(8,128)(2,1)} %param.18, f32[1024,1024]{1,0:T(8,128)} %fusion.67, bf16[2048,1024]{1,0:T(8,128)(2,1)} %param.17, f32[2048]{0:T(1024)S(1)} %convert_element_type.69, f32[1024]{0:T(1024)S(1)} %add_rsqrt_fusion.1), kind=kOutput, calls=%fused_computation.127 | convolution fusion | flops 8610906112 | bytes 25178116 | tf_op jit(solution)/shard_map/dot_general | solution.py:77
  36.9 4.0 fusion.103
  41.5 3.8 pad_maximum_fusion
  45.3 10.3 %all-to-all-start = ((f32[64,16,2048]{2,1,0:T(8,128)}), f32[64,16,2048]{2,1,0:T(8,128)}, u32[]{:S(2)}, u32[]{:S(2)}) async-start(f32[64,16,2048]{2,1,0:T(8,128)} %bitcast.71), calls=%async_computation | async-start | bytes 16777216 | tf_op jit(solution)/shard_map/all_to_all | solution.py:81
  55.7 106.3 %all-to-all-done = f32[64,16,2048]{2,1,0:T(8,128)} async-done(((f32[64,16,2048]{2,1,0:T(8,128)}), f32[64,16,2048]{2,1,0:T(8,128)}, u32[]{:S(2)}, u32[]{:S(2)}) %all-to-all-start) | async-done | bytes 8388640 | tf_op jit(solution)/shard_map/all_to_all | solution.py:81
  162.0 4.4 bitcast_reduce_fusion
  171.1 35.9 %all-gather.3.cloned.1.call-done = bf16[1024,2048]{1,0:T(8,128)(2,1)} async-done(((bf16[128,2048]{1,0:T(8,128)(2,1)}), bf16[1024,2048]{1,0:T(8,128)(2,1)}) %all-gather.3.cloned.1.call-update) | async-done | bytes 4194320 | tf_op jit(solution)/shard_map/all_gather | solution.py:91
  207.0 6.4 %fusion.60 = f32[1024,768]{0,1:T(8,128)S(1)} fusion(bf16[1024,2048]{1,0:T(8,128)(2,1)} %all-gather.3.cloned.1.call-done, bf16[2048,256]{1,0:T(8,128)(2,1)S(1)} %copy-done.8, bf16[2048,256]{1,0:T(8,128)(2,1)} %param.21, bf16[2048,256]{1,0:T(8,128)(2,1)} %param.20), kind=kOutput, calls=%fused_computation.133 | convolution fusion | flops 3230662656 | bytes 10485760 | tf_op jit(solution)/shard_map/dot_general | solution.py:94
  223.8 3.5 subtract_convert_fusion
  232.9 6.2 %gather_fusion.1 = s32[1024]{0:T(1024)S(1)} fusion(s32[8192]{0:T(1024)S(1)} %copy-done.1, s32[1024]{0:T(1024)S(1)} %broadcast_clamp_fusion.1), kind=kCustom, calls=%fused_computation.1 | custom fusion | bytes 12288 | tf_op jit(solution)/shard_map/gather | solution.py:105
  240.1 84.4 %all-gather.5.cloned.1.call-done = bf16[8192,512]{0,1:T(8,128)(2,1)} async-done(((bf16[1024,512]{0,1:T(8,128)(2,1)}), bf16[8192,512]{0,1:T(8,128)(2,1)}) %all-gather.5.cloned.1.call-update) | async-done | bytes 8388624 | tf_op jit(solution)/shard_map/all_gather | solution.py:112
  324.5 153.9 %while.18 = (s32[]{:T(128)}, f32[2,1024]{1,0:T(2,128)S(1)}, f32[2,1024]{1,0:T(2,128)S(1)}, f32[2,1024,128]{2,1,0:T(8,128)}, s32[8]{0:T(128)S(1)}, /*index=5*/s32...) while((s32[]{:T(128)}, f32[2,1024]{1,0:T(2,128)S(1)}, ...), condition=%wide.region_6.7_spmd.clone, body=%wide.region_3.6_spmd.clone.sunk | while | flops 1105164288 | bytes 45793624 | solution.py:145
  325.9 6.2 %gather_fusion = s32[1024]{0:T(1024)S(1)} fusion(s32[8192]{0:T(1024)S(1)} %get-tuple-element.404, s32[1024]{0:T(1024)S(1)} %broadcast_clamp_fusion.3), kind=kCustom, calls=%fused_computation.clone.clone.1 | custom fusion | bytes 12288 | tf_op jit(solution)/shard_map/while/body/eval_jaxpr/gather | solution.py:126
  338.9 3.7 fusion.137
  345.2 6.2 %gather_fusion = s32[1024]{0:T(1024)S(1)} fusion(s32[8192]{0:T(1024)S(1)} %get-tuple-element.404, s32[1024]{0:T(1024)S(1)} %broadcast_clamp_fusion.3), kind=kCustom, calls=%fused_computation.clone.clone.1 | custom fusion | bytes 12288 | tf_op jit(solution)/shard_map/while/body/eval_jaxpr/gather | solution.py:126
  358.2 3.7 fusion.137
  364.4 6.2 %gather_fusion = s32[1024]{0:T(1024)S(1)} fusion(s32[8192]{0:T(1024)S(1)} %get-tuple-element.404, s32[1024]{0:T(1024)S(1)} %broadcast_clamp_fusion.3), kind=kCustom, calls=%fused_computation.clone.clone.1 | custom fusion | bytes 12288 | tf_op jit(solution)/shard_map/while/body/eval_jaxpr/gather | solution.py:126
  377.4 3.7 fusion.137
  383.6 6.2 %gather_fusion = s32[1024]{0:T(1024)S(1)} fusion(s32[8192]{0:T(1024)S(1)} %get-tuple-element.404, s32[1024]{0:T(1024)S(1)} %broadcast_clamp_fusion.3), kind=kCustom, calls=%fused_computation.clone.clone.1 | custom fusion | bytes 12288 | tf_op jit(solution)/shard_map/while/body/eval_jaxpr/gather | solution.py:126
  396.6 3.7 fusion.137
  402.9 6.2 %gather_fusion = s32[1024]{0:T(1024)S(1)} fusion(s32[8192]{0:T(1024)S(1)} %get-tuple-element.404, s32[1024]{0:T(1024)S(1)} %broadcast_clamp_fusion.3), kind=kCustom, calls=%fused_computation.clone.clone.1 | custom fusion | bytes 12288 | tf_op jit(solution)/shard_map/while/body/eval_jaxpr/gather | solution.py:126
  415.9 3.7 fusion.137
  422.1 6.2 %gather_fusion = s32[1024]{0:T(1024)S(1)} fusion(s32[8192]{0:T(1024)S(1)} %get-tuple-element.404, s32[1024]{0:T(1024)S(1)} %broadcast_clamp_fusion.3), kind=kCustom, calls=%fused_computation.clone.clone.1 | custom fusion | bytes 12288 | tf_op jit(solution)/shard_map/while/body/eval_jaxpr/gather | solution.py:126
  435.1 3.7 fusion.137
  441.3 6.2 %gather_fusion = s32[1024]{0:T(1024)S(1)} fusion(s32[8192]{0:T(1024)S(1)} %get-tuple-element.404, s32[1024]{0:T(1024)S(1)} %broadcast_clamp_fusion.3), kind=kCustom, calls=%fused_computation.clone.clone.1 | custom fusion | bytes 12288 | tf_op jit(solution)/shard_map/while/body/eval_jaxpr/gather | solution.py:126
  454.4 3.7 fusion.137
  460.6 6.2 %gather_fusion = s32[1024]{0:T(1024)S(1)} fusion(s32[8192]{0:T(1024)S(1)} %get-tuple-element.404, s32[1024]{0:T(1024)S(1)} %broadcast_clamp_fusion.3), kind=kCustom, calls=%fused_computation.clone.clone.1 | custom fusion | bytes 12288 | tf_op jit(solution)/shard_map/while/body/eval_jaxpr/gather | solution.py:126
  473.6 3.7 fusion.137
  480.1 3.3 convolution_convert_fusion
  483.4 37.2 %reduce-scatter.2.cloned.1.call-done = bf16[128,2048]{1,0:T(8,128)(2,1)} async-done(((bf16[1024,2048]{1,0:T(8,128)(2,1)}), bf16[128,2048]{1,0:T(8,128)(2,1)}) %reduce-scatter.2.cloned.1.call-update) | async-done | bytes 524304 | tf_op jit(solution)/shard_map/reduce_scatter | solution.py:155
  (186 shorter events, 94.6 us)
Async XLA Ops:
  6.5 473.5 %copy-start = (bf16[256,2048]{1,0:T(8,128)(2,1)S(1)}, bf16[256,2048]{1,0:T(8,128)(2,1)}, u32[]{:S(2)}) copy-start(bf16[256,2048]{1,0:T(8,128)(2,1)} %param.23) | copy-start | bytes 3145732
  6.5 3.2 copy-start.6
  45.3 10.4 %copy-start.7 = (bf16[2048]{0:T(1024)(128)(2,1)S(1)}, bf16[2048]{0:T(1024)(128)(2,1)}, u32[]{:S(2)}) copy-start(bf16[2048]{0:T(1024)(128)(2,1)} %param.19) | copy-start | bytes 12292
  45.3 116.7 %all-to-all-start = ((f32[64,16,2048]{2,1,0:T(8,128)}), f32[64,16,2048]{2,1,0:T(8,128)}, u32[]{:S(2)}, u32[]{:S(2)}) async-start(f32[64,16,2048]{2,1,0:T(8,128)} %bitcast.71), calls=%async_computation | async-start | bytes 16777216 | tf_op jit(solution)/shard_map/all_to_all | solution.py:81
  55.6 151.3 %all-gather.3.cloned.1.call-start = ((), (), s32[]{:S(2)}) async-start(), calls=%async_computation.2 | async-start | bytes 4718592 | tf_op jit(solution)/shard_map/all_gather | solution.py:91
  55.7 151.3 %copy-start.8 = (bf16[2048,256]{1,0:T(8,128)(2,1)S(1)}, bf16[2048,256]{1,0:T(8,128)(2,1)}, u32[]{:S(2)}) copy-start(bf16[2048,256]{1,0:T(8,128)(2,1)} %param.22) | copy-start | bytes 3145732
  167.8 156.8 %all-gather.5.cloned.1.call-start = ((), (), s32[]{:S(2)}) async-start(), calls=%async_computation.3 | async-start | bytes 9437184 | tf_op jit(solution)/shard_map/all_gather | solution.py:112
  227.3 5.6 %copy-start.1 = (s32[8192]{0:T(1024)S(1)}, s32[8192]{0:T(1024)}, u32[]{:S(2)}) copy-start(s32[8192]{0:T(1024)} %param.14) | copy-start | bytes 98308
  228.4 10.7 %copy-start.2 = (bf16[1024,2,64]{2,0,1:T(8,128)(2,1)S(1)}, bf16[1024,2,64]{2,0,1:T(8,128)(2,1)}, u32[]{:S(2)}) copy-start(bf16[1024,2,64]{2,0,1:T(8,128)(2,1)} %get-tuple-element.271) | copy-start | bytes 786436
  232.7 287.8 %reduce-scatter.2.cloned.1.call-start = ((), (), s32[]{:S(2)}) async-start(), calls=%async_computation.4 | async-start | bytes 4718592 | tf_op jit(solution)/shard_map/reduce_scatter | solution.py:155
  324.5 10.1 %copy-start.5 = (bf16[1024,2,128]{2,0,1:T(8,128)(2,1)S(1)}, bf16[1024,2,128]{2,0,1:T(8,128)(2,1)}, u32[]{:S(2)}) copy-start(bf16[1024,2,128]{2,0,1:T(8,128)(2,1)} %get-tuple-element.407) | copy-start | bytes 1572868 | tf_op jit(solution)/shard_map/while
  336.6 2.3 copy-start.3
  342.7 1.1 copy-start.4
  343.8 10.1 %copy-start.5 = (bf16[1024,2,128]{2,0,1:T(8,128)(2,1)S(1)}, bf16[1024,2,128]{2,0,1:T(8,128)(2,1)}, u32[]{:S(2)}) copy-start(bf16[1024,2,128]{2,0,1:T(8,128)(2,1)} %get-tuple-element.407) | copy-start | bytes 1572868 | tf_op jit(solution)/shard_map/while
  355.9 2.3 copy-start.3
  361.9 1.1 copy-start.4
  363.0 10.1 %copy-start.5 = (bf16[1024,2,128]{2,0,1:T(8,128)(2,1)S(1)}, bf16[1024,2,128]{2,0,1:T(8,128)(2,1)}, u32[]{:S(2)}) copy-start(bf16[1024,2,128]{2,0,1:T(8,128)(2,1)} %get-tuple-element.407) | copy-start | bytes 1572868 | tf_op jit(solution)/shard_map/while
  375.1 2.3 copy-start.3
  381.2 1.1 copy-start.4
  382.2 10.1 %copy-start.5 = (bf16[1024,2,128]{2,0,1:T(8,128)(2,1)S(1)}, bf16[1024,2,128]{2,0,1:T(8,128)(2,1)}, u32[]{:S(2)}) copy-start(bf16[1024,2,128]{2,0,1:T(8,128)(2,1)} %get-tuple-element.407) | copy-start | bytes 1572868 | tf_op jit(solution)/shard_map/while
  394.3 2.3 copy-start.3
  400.4 1.1 copy-start.4
  401.5 10.1 %copy-start.5 = (bf16[1024,2,128]{2,0,1:T(8,128)(2,1)S(1)}, bf16[1024,2,128]{2,0,1:T(8,128)(2,1)}, u32[]{:S(2)}) copy-start(bf16[1024,2,128]{2,0,1:T(8,128)(2,1)} %get-tuple-element.407) | copy-start | bytes 1572868 | tf_op jit(solution)/shard_map/while
  413.6 2.3 copy-start.3
  419.6 1.1 copy-start.4
  420.7 10.1 %copy-start.5 = (bf16[1024,2,128]{2,0,1:T(8,128)(2,1)S(1)}, bf16[1024,2,128]{2,0,1:T(8,128)(2,1)}, u32[]{:S(2)}) copy-start(bf16[1024,2,128]{2,0,1:T(8,128)(2,1)} %get-tuple-element.407) | copy-start | bytes 1572868 | tf_op jit(solution)/shard_map/while
  432.8 2.3 copy-start.3
  438.9 1.1 copy-start.4
  439.9 10.1 %copy-start.5 = (bf16[1024,2,128]{2,0,1:T(8,128)(2,1)S(1)}, bf16[1024,2,128]{2,0,1:T(8,128)(2,1)}, u32[]{:S(2)}) copy-start(bf16[1024,2,128]{2,0,1:T(8,128)(2,1)} %get-tuple-element.407) | copy-start | bytes 1572868 | tf_op jit(solution)/shard_map/while
  452.0 2.3 copy-start.3
  459.2 10.1 %copy-start.5 = (bf16[1024,2,128]{2,0,1:T(8,128)(2,1)S(1)}, bf16[1024,2,128]{2,0,1:T(8,128)(2,1)}, u32[]{:S(2)}) copy-start(bf16[1024,2,128]{2,0,1:T(8,128)(2,1)} %get-tuple-element.407) | copy-start | bytes 1572868 | tf_op jit(solution)/shard_map/while
  471.3 2.3 copy-start.3
  (2 other events, 2.1 us)
Sparse Core Ops, SparseCore 0:
  167.9 39.0 all-gather.2
  232.9 91.6 all-gather.4
  483.5 37.0 reduce-scatter.1
where the time goes:
time: 530 us; the launch traced here: 529 us
  waiting for transfers between devices  264 us (50%)
  local copies, waits for them, and re-layouts  97.9 us (18%)
  matrix products  82.7 us (16%)
  other arithmetic  54.8 us (10%)
  between operations  13.3 us (3%)
  starting transfers between devices  10.6 us (2%)
  loops' own time  5.89 us (1%)
    all_to_all x1, waiting for transfers between devices, body(): lax.all_to_all(outgoing, ('seq', 'tensor'), split_axis=0, concat_axis=0,...  106 us
    all_gather x1, waiting for transfers between devices, body(): shard_piece = lax.all_gather(key_values, 'seq', axis=0, tiled=True)  84.4 us
    gather x8, local copies, waits for them, and re-layouts, one_step(): doc_ids[key_pos][None, :] == query_docs[:, None]  49.2 us
    reduce_scatter x1, waiting for transfers between devices, body(): lax.psum_scatter(jnp.dot(context, out_weight, preferred_element_type=jnp....  37.2 us
    all_gather x1, waiting for transfers between devices, body(): shard_piece = lax.all_gather(attn_in, 'tensor', axis=0, tiled=True)  35.9 us
    dot_general x8, matrix products, one_step(): jnp.einsum('hqk,khd->hqd', weights.astype(jnp.bfloat16), value_block, pre...  30 us
    reduce_sum x8, other arithmetic, one_step(): running_sum = running_sum * rescale + jnp.sum(weights, axis=2)  18.1 us
    dot_general x1, matrix products, body(): jnp.dot(hidden, down_weight, preferred_element_type=jnp.float32)  17.2 us
  transfers between devices with their start and end apart: 4, of which 4 were waited for; matrix products, arithmetic and copies ran while one was open for 2% of the time, Pallas kernels for 0%

commit v1 on v0

v1 whole, which is shorter than its diff:
```python
import functools

import jax
import jax.numpy as jnp
import numpy as np
from jax import lax
from jax.experimental import pallas as pl
from jax.experimental.pallas import tpu as pltpu
from jax.sharding import PartitionSpec as P

HEAD_DIM = 128
EPSILON = 1e-05
ROPE_BASE = 500000.0
NEGATIVE = -1e30
MESH = pl.DeviceIdType.MESH
F32 = jnp.float32
BF16 = jnp.bfloat16
VMEM_LIMIT = 60 * 1024 * 1024


def place():
    s = lax.axis_index("seq")
    c = lax.axis_index("tensor")
    return s, c, s // 4, s % 4, c // 2, c % 2


def remote(src, dst, send_sem, recv_sem, seq, tensor):
    return pltpu.make_async_remote_copy(
        src_ref=src,
        dst_ref=dst,
        send_sem=send_sem,
        recv_sem=recv_sem,
        device_id={"dp": lax.axis_index("dp"), "seq": seq, "tensor": tensor},
        device_id_type=MESH,
    )


def arrived(dst, recv_sem):
    pltpu.make_async_copy(dst, dst, recv_sem).wait()


def greet(partners):
    barrier = pltpu.get_barrier_semaphore()
    for seq, tensor in partners:
        pl.semaphore_signal(
            barrier,
            inc=1,
            device_id={"dp": lax.axis_index("dp"), "seq": seq, "tensor": tensor},
            device_id_type=MESH,
        )
    pl.semaphore_wait(barrier, len(partners))


def normalized(values, gain):
    mean_square = jnp.mean(values * values, axis=-1, keepdims=True)
    return (values * lax.rsqrt(mean_square + EPSILON) * gain).astype(BF16)


class RingSum:
    def __init__(self, send, recv, send_sem, recv_sem, s, z, k):
        self.send, self.recv = send, recv
        self.send_sem, self.recv_sem = send_sem, recv_sem
        self.s, self.z = s, z
        self.up = (z + 1) % 4
        self.down = (z + 3) % 4
        self.far = (z + 2) % 4
        self.up_c = self.up * 2 + k
        self.down_c = self.down * 2 + k

    def copies(self, ch, phase):
        part = pl.ds(0, 2) if phase == 0 else pl.ds(2, 1)
        made = []
        for d, target in ((0, self.up_c), (1, self.down_c)):
            made.append(
                remote(
                    self.send.at[ch, d, part],
                    self.recv.at[ch, d, part],
                    self.send_sem.at[ch, d, phase],
                    self.recv_sem.at[ch, d, phase],
                    self.s,
                    target,
                )
            )
        return made

    def first(self, ch, value):
        self.send[ch, 0, 0] = value(self.far, 0).astype(BF16)
        self.send[ch, 0, 1] = value(self.up, 1).astype(BF16)
        self.send[ch, 1, 0] = value(self.far, 1).astype(BF16)
        self.send[ch, 1, 1] = value(self.down, 0).astype(BF16)
        for copy in self.copies(ch, 0):
            copy.start()

    def second(self, ch, value):
        for copy in self.copies(ch, 0):
            copy.wait_recv()
        self.send[ch, 0, 2] = (value(self.up, 0) + self.recv[ch, 0, 0].astype(F32)).astype(BF16)
        self.send[ch, 1, 2] = (value(self.down, 1) + self.recv[ch, 1, 0].astype(F32)).astype(BF16)
        for copy in self.copies(ch, 1):
            copy.start()

    def third(self, ch, value):
        for copy in self.copies(ch, 1):
            copy.wait_recv()
        one = (
            value(self.z, 0)
            + self.recv[ch, 0, 2].astype(F32)
            + self.recv[ch, 1, 1].astype(F32)
        )
        two = (
            value(self.z, 1)
            + self.recv[ch, 0, 1].astype(F32)
            + self.recv[ch, 1, 2].astype(F32)
        )
        return one, two

    def finish(self, ch):
        for phase in range(2):
            for copy in self.copies(ch, phase):
                copy.wait_send()


def ff_kernel(
    tok_hbm, gain_ref, wg_hbm, wu_hbm, wd_hbm, q_hbm, k_hbm, v_hbm, o_hbm,
    stream_ref, sq_hbm, sk_hbm, sv_hbm, so_hbm,
    tok, wg, wu, wd, xn, hid, mine, csend, crecv, zsend, zrecv, sstage,
    tok_sem, gu_sem, wd_sem, wsem_s, wsem_r, csem_s, csem_r, zsem_s, zsem_r, ssem_s, ssem_r, own_sem,
):
    s, c, y, x, z, k = place()
    sib = c + 1 - 2 * k
    ff = wg.shape[1]
    width = tok.shape[1]
    gu_tiles = 4
    gu_cols = ff // gu_tiles

    def pair_of(ch):
        return (s // 2 + 1 + ch) % 4

    def tok_copies(ch):
        a = pair_of(ch) * 2
        low = pl.ds(pl.multiple_of(a * 64, 128), 128)
        high = pl.ds(pl.multiple_of((14 - a) * 64, 128), 128)
        return [
            pltpu.make_async_copy(tok_hbm.at[low], tok.at[low], tok_sem.at[ch, 0]),
            pltpu.make_async_copy(tok_hbm.at[high], tok.at[high], tok_sem.at[ch, 1]),
        ]

    def gu_copies(n):
        cols = pl.ds(n * gu_cols, gu_cols)
        return [
            pltpu.make_async_copy(wg_hbm.at[:, cols], wg.at[:, cols], gu_sem.at[n, 0]),
            pltpu.make_async_copy(wu_hbm.at[:, cols], wu.at[:, cols], gu_sem.at[n, 1]),
        ]

    wd_copy = pltpu.make_async_copy(wd_hbm, wd, wd_sem.at[0])
    for copy in tok_copies(0):
        copy.start()
    for n in range(gu_tiles):
        for copy in gu_copies(n):
            copy.start()
    wd_copy.start()
    for ch in range(1, 4):
        for copy in tok_copies(ch):
            copy.start()

    ring = RingSum(zsend, zrecv, zsem_s, zsem_r, s, z, k)
    partners = [(s, sib), (s, ring.up_c), (s, ring.down_c)]
    partners += [((s + d) % 8, c) for d in range(1, 8)]
    greet(partners)

    weight_sends = [
        remote(src, dst, wsem_s.at[i], wsem_r.at[i], s, sib)
        for i, (src, dst) in enumerate(
            ((q_hbm, sq_hbm), (k_hbm, sk_hbm), (v_hbm, sv_hbm), (o_hbm, so_hbm))
        )
    ]

    def token_rows(ch):
        a = pair_of(ch) * 2
        low = tok[pl.ds(pl.multiple_of(a * 64, 128), 128), :]
        high = tok[pl.ds(pl.multiple_of((14 - a) * 64, 128), 128), :]
        return low, high

    def gate_tile(cols):
        gate = jnp.dot(xn[...], wg[:, cols], preferred_element_type=F32)
        up = jnp.dot(xn[...], wu[:, cols], preferred_element_type=F32)
        hid[:, cols] = (gate / (1.0 + jnp.exp(-gate)) * up).astype(BF16)

    def hidden(ch):
        for copy in tok_copies(ch):
            copy.wait()
        low, high = token_rows(ch)
        gain = gain_ref[...].astype(F32)
        xn[0:128, :] = normalized(low.astype(F32), gain)
        xn[128:256, :] = normalized(high.astype(F32), gain)
        if ch == 0:
            for n in range(gu_tiles):
                for copy in gu_copies(n):
                    copy.wait()
                gate_tile(pl.ds(n * gu_cols, gu_cols))
        else:

            @pl.loop(0, gu_tiles)
            def _(n):
                gate_tile(pl.ds(pl.multiple_of(n * gu_cols, gu_cols), gu_cols))

    def core_copy(ch):
        return remote(csend.at[ch], crecv.at[ch], csem_s.at[ch], csem_r.at[ch], s, sib)

    def down(ch):
        if ch == 0:
            wd_copy.wait()
        cols_n = 256

        @pl.loop(0, width // cols_n)
        def _(n):
            cols = pl.ds(pl.multiple_of(n * cols_n, cols_n), cols_n)
            part = jnp.dot(hid[...], wd[:, cols], preferred_element_type=F32)
            part = part.reshape(4, 2, 2, 16, cols_n)
            even, odd = part[:, :, 0], part[:, :, 1]
            mine[ch, :, :, :, cols] = jnp.where(k == 0, even, odd)
            csend[ch, :, :, :, cols] = jnp.where(k == 0, odd, even).astype(BF16)

        core_copy(ch).start()

    def piece(ch):
        def value(zd, t):
            block = jnp.where(zd < 2, t, 3 - t)
            return mine[ch, block, zd % 2] + crecv[ch, block, zd % 2].astype(F32)

        return value

    def first(ch):
        core_copy(ch).wait_recv()
        ring.first(ch, piece(ch))

    def second(ch):
        ring.second(ch, piece(ch))

    def seq_copy(ch, t, target):
        return remote(
            sstage.at[ch, t], stream_ref.at[s], ssem_s.at[ch, t], ssem_r.at[s], target, c
        )

    def third(ch):
        totals = ring.third(ch, piece(ch))
        a = pair_of(ch) * 2
        for t in range(2):
            block = jnp.where(z < 2, a + t, 15 - a - t)
            start = pl.multiple_of(block * 64 + (2 * (z % 2) + k) * 16, 16)
            rows = tok[pl.ds(start, 16), :].astype(F32)
            sstage[ch, t] = (totals[t] + rows).astype(BF16)
            if ch < 3:
                seq_copy(ch, t, a + t).start()
            else:

                @pl.when(s == a + t)
                def _():
                    pltpu.make_async_copy(sstage.at[ch, t], stream_ref.at[s], own_sem.at[0]).start()

                @pl.when(s != a + t)
                def _():
                    seq_copy(ch, t, a + t).start()

    hidden(0)
    down(0)
    for copy in weight_sends:
        copy.start()
    hidden(1)
    first(0)
    down(1)
    hidden(2)
    first(1)
    second(0)
    down(2)
    hidden(3)
    first(2)
    second(1)
    third(0)
    down(3)
    second(2)
    third(1)
    first(3)
    third(2)
    second(3)
    third(3)

    for ch in range(4):
        core_copy(ch).wait_send()
        ring.finish(ch)
        a = pair_of(ch) * 2
        for t in range(2):
            if ch < 3:
                seq_copy(ch, t, a + t).wait_send()
            else:

                @pl.when(s == a + t)
                def _():
                    pltpu.make_async_copy(sstage.at[ch, t], stream_ref.at[s], own_sem.at[0]).wait()

                @pl.when(s != a + t)
                def _():
                    seq_copy(ch, t, a + t).wait_send()

    for d in range(1, 8):
        g = (s + d) % 8
        arrived(stream_ref.at[g], ssem_r.at[g])
    for copy in weight_sends:
        copy.wait()


def rope_table(groups, base_rows):
    half = HEAD_DIM // 2
    frequency = ROPE_BASE ** (-(np.arange(half, dtype=np.float64) / half))
    angles = np.arange(groups * base_rows, dtype=np.float64)[:, None] * frequency[None, :]
    cosine, sine = np.cos(angles), np.sin(angles)
    table = np.concatenate([cosine, cosine, -sine, sine], axis=1).astype(np.float32)
    return table.reshape(groups, 16, 2, 2, 16, 4 * half)


def qkv_kernel(
    stream_ref, gain_ref, q_hbm, k_hbm, v_hbm, sq_hbm, sk_hbm, sv_hbm, table_hbm,
    q_out, kv_out,
    xg, w, tab, qst, kvst,
    w_sem, tab_sem,
    own_s, own_r, relay_s, relay_r, q_s, q_r, kv_s, kv_r, yf_s, yf_r, f1_s, f1_r, f2_s, f2_r,
):
    s, c, y, x, z, k = place()
    sib = c + 1 - 2 * k
    up_c = ((z + 1) % 4) * 2 + k
    down_c = ((z + 3) % 4) * 2 + k
    up, down, far = (z + 1) % 4, (z + 3) % 4, (z + 2) % 4
    other_s = (1 - y) * 4 + x

    weight_copies = [
        pltpu.make_async_copy(src, w.at[i], w_sem.at[i])
        for i, src in enumerate((q_hbm, k_hbm, v_hbm, sq_hbm, sk_hbm, sv_hbm))
    ]
    table_copies = [
        pltpu.make_async_copy(
            table_hbm.at[:, jnp.where(half == 0, s, 15 - s) if half else s, :, k],
            tab.at[:, half],
            tab_sem.at[half],
        )
        for half in range(2)
    ]
    for copy in weight_copies + table_copies:
        copy.start()

    gain = gain_ref[...].astype(F32)
    xg[:, z] = normalized(stream_ref[...].astype(F32), gain)

    partners = [(s, sib), (s, up_c), (s, down_c), (other_s, c)]
    for d in range(1, 4):
        peer = y * 4 + (x + d) % 4
        partners += [(peer, c), (peer, sib)]
    greet(partners)

    def own_copies(jj):
        rows = pl.ds(2 * jj, 2)
        return [
            remote(xg.at[rows, z], xg.at[rows, z], own_s.at[jj, d], own_r.at[jj, d], s, target)
            for d, target in ((0, up_c), (1, down_c))
        ]

    def own_wait(jj):
        rows = pl.ds(2 * jj, 2)
        arrived(xg.at[rows, down], own_r.at[jj, 0])
        arrived(xg.at[rows, up], own_r.at[jj, 1])

    def relay_copies(jj):
        made = []
        for d, source, target in ((0, down, up_c), (1, up, down_c)):
            row = 2 * jj + d
            made.append(
                remote(
                    xg.at[row, source], xg.at[row, source],
                    relay_s.at[jj, d], relay_r.at[jj, d], s, target,
                )
            )
        return made

    def relay_wait(jj):
        for d in range(2):
            arrived(xg.at[2 * jj + d, far], relay_r.at[jj, d])

    core_of_rows = x // 2

    def q_sends(jj, d):
        hx = (x + d) % 4
        rows = pl.ds(4 * jj, 4)
        src = qst.at[jj, hx]
        dst = q_out.at[rows, x % 2, :, k]
        recv = q_r.at[jj, x % 2, k]
        far_copy = remote(src, dst, q_s.at[jj, d], recv, y * 4 + hx, z * 2 + core_of_rows)
        near_copy = pltpu.make_async_copy(src, dst, recv)
        return far_copy, near_copy

    def kv_send(jj, d):
        hx = (x + d) % 4
        rows = pl.ds(4 * jj, 4)
        src = kvst.at[jj, hx]
        dst = kv_out.at[rows, s, :, k]
        recv = kv_r.at[jj, x]
        if d == 0:
            return pltpu.make_async_copy(src, dst, recv)
        return remote(src, dst, kv_s.at[jj, d], recv, y * 4 + hx, c)

    def y_forward(jj, d):
        a = y * 4 + (x + d) % 4
        rows = pl.ds(4 * jj, 4)
        part = kv_out.at[rows, a, :, k]
        src = kvst.at[jj, x] if d == 0 else part
        return remote(src, part, yf_s.at[jj, d], yf_r.at[jj, (x + d) % 4], other_s, c)

    def core_forward(jj, which):
        first = y * 4 if which == 0 else (1 - y) * 4
        part = kv_out.at[pl.ds(4 * jj, 4), pl.ds(first, 4), :, k]
        send, recv = (f1_s, f1_r) if which == 0 else (f2_s, f2_r)
        return remote(part, part, send.at[jj], recv.at[jj], s, sib)

    def rope(values, cosine, sine):
        return values * cosine + pltpu.roll(values, HEAD_DIM // 2, 1) * sine

    def compute(jj):
        rows = pl.ds(2 * jj, 2)
        lhs = xg[rows].reshape(128, xg.shape[-1])
        trig = tab[rows].reshape(128, 2 * HEAD_DIM)
        cosine, sine = trig[:, :HEAD_DIM], trig[:, HEAD_DIM:]
        for part in range(2):
            core = k if part == 0 else 1 - k
            if jj == 0:
                for i in range(3):
                    weight_copies[3 * part + i].wait()
            qf = jnp.dot(lhs, w[3 * part], preferred_element_type=F32)
            kf = jnp.dot(lhs, w[3 * part + 1], preferred_element_type=F32)
            vf = jnp.dot(lhs, w[3 * part + 2], preferred_element_type=F32)
            for hh in range(2):
                cols = slice(hh * HEAD_DIM, (hh + 1) * HEAD_DIM)
                hx = 2 * core + hh
                qst[jj, hx] = rope(qf[:, cols], cosine, sine).astype(BF16).reshape(4, 2, 16, HEAD_DIM)
                kvst[jj, hx, :, :, :, :HEAD_DIM] = (
                    rope(kf[:, cols], cosine, sine).astype(BF16).reshape(4, 2, 16, HEAD_DIM)
                )
                kvst[jj, hx, :, :, :, HEAD_DIM:] = vf[:, cols].astype(BF16).reshape(4, 2, 16, HEAD_DIM)

    def send_out(jj):
        for d in (2, 1, 3, 0):
            kv_send(jj, d).start()
            if d == 0:
                y_forward(jj, 0).start()
        for d in (2, 1, 3, 0):
            far_copy, near_copy = q_sends(jj, d)
            if d == 0:

                @pl.when(core_of_rows == k)
                def _():
                    near_copy.start()

                @pl.when(core_of_rows != k)
                def _():
                    far_copy.start()
            else:
                far_copy.start()

    def forward_one(jj):
        rows = pl.ds(4 * jj, 4)
        for d in (1, 3, 2, 0):
            a = y * 4 + (x + d) % 4
            arrived(kv_out.at[rows, a, :, k], kv_r.at[jj, (x + d) % 4])
            if d:
                y_forward(jj, d).start()
        core_forward(jj, 0).start()

    def forward_two(jj):
        rows = pl.ds(4 * jj, 4)
        for xs in range(4):
            arrived(kv_out.at[rows, (1 - y) * 4 + xs, :, k], yf_r.at[jj, xs])
        core_forward(jj, 1).start()

    def start_own(jj):
        for copy in own_copies(jj):
            copy.start()

    def start_relay(jj):
        own_wait(jj)
        for copy in relay_copies(jj):
            copy.start()

    start_own(0)
    start_own(1)
    for copy in table_copies:
        copy.wait()
    start_relay(0)
    start_own(2)
    start_relay(1)
    start_own(3)
    relay_wait(0)
    compute(0)
    send_out(0)
    start_relay(2)
    relay_wait(1)
    compute(1)
    send_out(1)
    start_relay(3)
    forward_one(0)
    relay_wait(2)
    compute(2)
    send_out(2)
    forward_one(1)
    relay_wait(3)
    compute(3)
    send_out(3)
    forward_two(0)
    forward_one(2)
    forward_two(1)
    forward_one(3)
    forward_two(2)
    forward_two(3)

    for jj in range(4):
        rows = pl.ds(4 * jj, 4)
        for copy in own_copies(jj) + relay_copies(jj):
            copy.wait_send()
        for d in range(4):
            if d:
                kv_send(jj, d).wait_send()
            y_forward(jj, d).wait_send()
            far_copy, near_copy = q_sends(jj, d)
            if d == 0:

                @pl.when(core_of_rows != k)
                def _():
                    far_copy.wait_send()
            else:
                far_copy.wait_send()
        for which in range(2):
            core_forward(jj, which).wait_send()
        for aa in range(2):
            for kk in range(2):
                arrived(q_out.at[rows, aa, :, kk], q_r.at[jj, aa, kk])
        arrived(kv_out.at[rows, pl.ds(y * 4, 4), :, 1 - k], f1_r.at[jj])
        arrived(kv_out.at[rows, pl.ds((1 - y) * 4, 4), :, 1 - k], f2_r.at[jj])


def attention_kernel(info_ref, q_ref, kv_ref, out_ref, *, chunks, tile):
    log2e = 1.4426950408889634
    factor = HEAD_DIM ** (-0.5) * log2e
    half_rows = tile // 4
    first_block = info_ref[3]

    def row_start(position):
        start = jnp.zeros_like(position)
        for d in range(3):
            start = jnp.where(info_ref[d] <= position, info_ref[d], start)
        return start

    def low_first(g):
        return g * (2 * tile) + first_block * 64

    def high_first(g):
        return g * (2 * tile) + (14 - first_block) * 64

    def low_positions(g):
        row = lax.broadcasted_iota(jnp.int32, (128, 1), 0)
        return low_first(g) + row

    def high_positions(g):
        row = lax.broadcasted_iota(jnp.int32, (128, 1), 0)
        return high_first(g) + jnp.where(row < 64, row + 64, row - 64)

    def key_positions(t):
        col = lax.broadcasted_iota(jnp.int32, (1, tile), 1)
        flipped = (tile // 64 - 1 - col // 64) * 64 + col % 64
        return t * tile + jnp.where(t % 2 == 0, col, flipped)

    def update(state, queries, t, allowed):
        highest, total, weighted = state
        keys = kv_ref[t, :, :HEAD_DIM]
        scores = lax.dot_general(
            queries, keys, (((1,), (1,)), ((), ())), preferred_element_type=F32
        ) * factor
        if allowed is not None:
            scores = jnp.where(allowed, scores, NEGATIVE)
        new_highest = jnp.maximum(highest, jnp.max(scores, axis=1, keepdims=True))
        weights = jnp.exp2(scores - new_highest)
        if allowed is not None:
            weights = jnp.where(allowed, weights, 0.0)
        rescale = jnp.exp2(highest - new_highest)
        total = total * rescale + jnp.sum(weights, axis=1, keepdims=True)
        weighted = weighted * rescale + jnp.dot(
            weights.astype(BF16), kv_ref[t, :, HEAD_DIM:], preferred_element_type=F32
        )
        return new_highest, total, weighted

    def one_chunk(g, carry):
        queries = q_ref[pl.ds(2 * g, 2)].reshape(256, HEAD_DIM)
        positions = jnp.concatenate([low_positions(g), high_positions(g)], axis=0)
        starts = row_start(positions)
        first_tile = row_start(low_first(g)) // tile
        last_start = row_start(high_first(g) + 127)
        plain_tile = jnp.clip((last_start + tile - 1) // tile, first_tile, 2 * g)

        def masked_step(t, state):
            where_keys = key_positions(t)
            allowed = (where_keys <= positions) & (where_keys >= starts)
            return update(state, queries, t, allowed)

        def plain_step(t, state):
            return update(state, queries, t, None)

        state = (
            jnp.full((256, 1), NEGATIVE, F32),
            jnp.zeros((256, 1), F32),
            jnp.zeros((256, HEAD_DIM), F32),
        )
        state = lax.fori_loop(first_tile, plain_tile, masked_step, state)
        state = lax.fori_loop(plain_tile, 2 * g, plain_step, state)
        highest, total, weighted = masked_step(2 * g, state)
        out_ref[2 * g] = (weighted[:128] / total[:128]).astype(BF16)
        t = 2 * g + 1
        where_keys = key_positions(t)
        allowed = (where_keys <= positions[128:]) & (where_keys >= starts[128:])
        highest, total, weighted = update(
            (highest[128:], total[128:], weighted[128:]), queries[128:], t, allowed
        )
        out_ref[t] = (weighted / total).astype(BF16)
        return carry

    lax.fori_loop(0, chunks, one_chunk, 0)


def out_kernel(
    ctx_ref, stream_ref, o_hbm, so_hbm,
    out_ref,
    cbuf, w, mine, zsend, zrecv,
    w_sem, x_s, x_r, zsem_s, zsem_r,
):
    s, c, y, x, z, k = place()
    sib = c + 1 - 2 * k
    weight_copies = [
        pltpu.make_async_copy(src, w.at[i], w_sem.at[i]) for i, src in enumerate((o_hbm, so_hbm))
    ]
    for copy in weight_copies:
        copy.start()
    ring = RingSum(zsend, zrecv, zsem_s, zsem_r, s, z, k)
    partners = [(s, sib), (s, ring.up_c), (s, ring.down_c)]
    for d in range(1, 4):
        peer = y * 4 + (x + d) % 4
        partners += [(peer, c), (peer, sib)]
    greet(partners)

    def x_copies(jj, aa, kk):
        target_x = 2 * k + aa
        src = ctx_ref.at[pl.ds(4 * jj, 4), aa, :, kk]
        dst = cbuf.at[x, pl.ds(4 * jj, 4)]
        recv = x_r.at[jj, x]
        far_copy = remote(src, dst, x_s.at[jj, aa, kk], recv, y * 4 + target_x, z * 2 + kk)
        near_copy = pltpu.make_async_copy(src, dst, recv)
        return far_copy, near_copy, (target_x == x) & (k == kk)

    for jj in range(4):
        for aa in range(2):
            for kk in range(2):
                far_copy, near_copy, here = x_copies(jj, aa, kk)

                @pl.when(here)
                def _():
                    near_copy.start()

                @pl.when(jnp.logical_not(here))
                def _():
                    far_copy.start()

    width = w.shape[-1]
    cols_n = 512

    def compute(jj):
        rows = pl.ds(4 * jj, 4)
        for xs in range(4):
            arrived(cbuf.at[xs, rows], x_r.at[jj, xs])
        if jj == 0:
            for copy in weight_copies:
                copy.wait()

        def side(core):
            return jnp.concatenate(
                [cbuf[2 * core + hh, rows].reshape(128, HEAD_DIM) for hh in range(2)], axis=1
            )

        own, other = side(k), side(1 - k)

        @pl.loop(0, width // cols_n)
        def _(n):
            cols = pl.ds(pl.multiple_of(n * cols_n, cols_n), cols_n)
            part = jnp.dot(own, w[0, :, cols], preferred_element_type=F32)
            part += jnp.dot(other, w[1, :, cols], preferred_element_type=F32)
            mine[jj, :, :, :, cols] = part.reshape(2, 4, 16, cols_n)

    def piece(jj):
        def value(zd, t):
            return mine[jj, t, zd]

        return value

    def third(jj):
        totals = ring.third(jj, piece(jj))
        for t in range(2):
            g = 2 * jj + t
            out_ref[g] = (totals[t] + stream_ref[g].astype(F32)).astype(BF16)

    compute(0)
    ring.first(0, piece(0))
    compute(1)
    ring.first(1, piece(1))
    ring.second(0, piece(0))
    compute(2)
    ring.first(2, piece(2))
    ring.second(1, piece(1))
    compute(3)
    ring.first(3, piece(3))
    third(0)
    ring.second(2, piece(2))
    third(1)
    ring.second(3, piece(3))
    third(2)
    third(3)

    for jj in range(4):
        ring.finish(jj)
        for aa in range(2):
            for kk in range(2):
                far_copy, near_copy, here = x_copies(jj, aa, kk)

                @pl.when(jnp.logical_not(here))
                def _():
                    far_copy.wait_send()


ANY = pl.BlockSpec(memory_space=pl.ANY)
VM = pl.BlockSpec(memory_space=pltpu.VMEM)
SM = pl.BlockSpec(memory_space=pltpu.SMEM)
DMA = pltpu.SemaphoreType.DMA


def params(collective_id):
    return pltpu.CompilerParams(
        collective_id=collective_id, has_side_effects=True, vmem_limit_bytes=VMEM_LIMIT
    )


def like(array):
    return jax.ShapeDtypeStruct(array.shape, array.dtype)


def feed_forward(tokens, gain, gate, up, down, query, key, value, out):
    rows, width = tokens.shape
    ff = gate.shape[1]
    return pl.pallas_call(
        ff_kernel,
        name="feed_forward",
        out_shape=[
            jax.ShapeDtypeStruct((8, 16, width), BF16), like(query), like(key), like(value), like(out),
        ],
        in_specs=[ANY, VM] + [ANY] * 7,
        out_specs=[ANY] * 5,
        scratch_shapes=[
            pltpu.VMEM((rows, width), BF16),
            pltpu.VMEM((width, ff), BF16),
            pltpu.VMEM((width, ff), BF16),
            pltpu.VMEM((ff, width), BF16),
            pltpu.VMEM((256, width), BF16),
            pltpu.VMEM((256, ff), BF16),
            pltpu.VMEM((4, 4, 2, 16, width), F32),
            pltpu.VMEM((4, 4, 2, 16, width), BF16),
            pltpu.VMEM((4, 4, 2, 16, width), BF16),
            pltpu.VMEM((4, 2, 3, 16, width), BF16),
            pltpu.VMEM((4, 2, 3, 16, width), BF16),
            pltpu.VMEM((4, 2, 16, width), BF16),
            DMA((4, 2)), DMA((4, 2)), DMA((1,)), DMA((4,)), DMA((4,)), DMA((4,)), DMA((4,)),
            DMA((4, 2, 2)), DMA((4, 2, 2)), DMA((4, 2)), DMA((8,)), DMA((1,)),
        ],
        compiler_params=params(1),
    )(tokens, gain.reshape(1, width), gate, up, down, query, key, value, out)


def project(stream, gain, own, other, table):
    width = stream.shape[-1]
    cols = own[0].shape[1]
    return pl.pallas_call(
        qkv_kernel,
        name="project",
        out_shape=[
            jax.ShapeDtypeStruct((16, 2, 2, 2, 16, HEAD_DIM), BF16),
            jax.ShapeDtypeStruct((16, 8, 2, 2, 16, 2 * HEAD_DIM), BF16),
        ],
        in_specs=[VM, VM] + [ANY] * 7,
        out_specs=[ANY] * 2,
        scratch_shapes=[
            pltpu.VMEM((8, 4, 16, width), BF16),
            pltpu.VMEM((6, width, cols), BF16),
            pltpu.VMEM((8, 2, 2, 16, 2 * HEAD_DIM), F32),
            pltpu.VMEM((4, 4, 4, 2, 16, HEAD_DIM), BF16),
            pltpu.VMEM((4, 4, 4, 2, 16, 2 * HEAD_DIM), BF16),
            DMA((6,)), DMA((2,)),
            DMA((4, 2)), DMA((4, 2)), DMA((4, 2)), DMA((4, 2)),
            DMA((4, 4)), DMA((4, 2, 2)), DMA((4, 4)), DMA((4, 4)),
            DMA((4, 4)), DMA((4, 4)), DMA((4,)), DMA((4,)), DMA((4,)), DMA((4,)),
        ],
        compiler_params=params(2),
    )(stream, gain.reshape(1, width), *own, *other, table)


def attend(info, queries, keys_values):
    tiles = keys_values.shape[0]
    tile = keys_values.shape[1]
    return pl.pallas_call(
        functools.partial(attention_kernel, chunks=tiles // 2, tile=tile),
        name="attend",
        out_shape=like(queries),
        in_specs=[SM, VM, VM],
        out_specs=VM,
        compiler_params=pltpu.CompilerParams(vmem_limit_bytes=VMEM_LIMIT),
    )(info, queries, keys_values)


def merge(context, stream, own, other):
    width = stream.shape[-1]
    return pl.pallas_call(
        out_kernel,
        name="merge",
        out_shape=like(stream),
        in_specs=[ANY, VM, ANY, ANY],
        out_specs=VM,
        scratch_shapes=[
            pltpu.VMEM((4, 16, 2, 16, HEAD_DIM), BF16),
            pltpu.VMEM((2,) + own.shape, BF16),
            pltpu.VMEM((4, 2, 4, 16, width), F32),
            pltpu.VMEM((4, 2, 3, 16, width), BF16),
            pltpu.VMEM((4, 2, 3, 16, width), BF16),
            DMA((2,)), DMA((4, 2, 2)), DMA((4, 4)), DMA((4, 2, 2)), DMA((4, 2, 2)),
        ],
        compiler_params=params(3),
    )(context, stream, own, other)


def body(
    tokens, doc_ids, mlp_gain, gate_weight, up_weight, down_weight,
    attn_gain, query_weight, key_weight, value_weight, out_weight,
):
    s = lax.axis_index("seq")
    k = lax.axis_index("tensor") % 2
    starts = jnp.sum(
        (doc_ids[None, :] < jnp.arange(1, 4, dtype=jnp.int32)[:, None]).astype(jnp.int32), axis=1
    )
    first_block = (s // 4) * 4 + 2 * k
    info = jnp.concatenate([starts, first_block[None].astype(jnp.int32)])
    stream, sq, sk, sv, so = feed_forward(
        tokens, mlp_gain, gate_weight, up_weight, down_weight,
        query_weight, key_weight, value_weight, out_weight,
    )
    table = jnp.asarray(rope_table(8, tokens.shape[0]))
    queries, keys_values = project(
        stream, attn_gain, (query_weight, key_weight, value_weight), (sq, sk, sv), table
    )
    context = attend(
        info, queries.reshape(16, 128, HEAD_DIM), keys_values.reshape(16, 512, 2 * HEAD_DIM)
    )
    merged = merge(context.reshape(16, 2, 2, 2, 16, HEAD_DIM), stream, out_weight, so)
    return merged.reshape(128, tokens.shape[1])


def solution(mesh):
    in_specs = (
        P(("dp", "seq"), None),
        P("dp"),
        P(),
        P(None, "tensor"),
        P(None, "tensor"),
        P("tensor", None),
        P(),
        P(None, "tensor"),
        P(None, "tensor"),
        P(None, "tensor"),
        P("tensor", None),
    )
    out_specs = P(("dp", "seq", "tensor"), None)
    return jax.shard_map(body, mesh=mesh, in_specs=in_specs, out_specs=out_specs, check_vma=False)
```

time: 530 us -> 153 us (0.29)
  waiting for transfers between devices: 264 us -> 0 us
  Pallas kernels: 0 us -> 144 us
  local copies, waits for them, and re-layouts: 97.9 us -> 4.46 us
  matrix products: 82.7 us -> 0 us
  other arithmetic: 54.8 us -> 1.67 us
  between operations: 13.3 us -> 0.03 us
  starting transfers between devices: 10.6 us -> 0 us
  loops' own time: 5.89 us -> 0 us
    pallas_call x0 -> x4, Pallas kernels: none -> 144 us  [the longest x1 48.4 us: feed_forward(): pl.pallas_call(ff_kernel, name='feed_forward', out_shape=[jax.ShapeDtypeS...]
    all_gather x2 -> x0, waiting for transfers between devices: 120 us -> none  [the longest x1 84.4 us: body(): shard_piece = lax.all_gather(key_values, 'seq', axis=0, tiled=True)]
    all_to_all x1 -> x0, waiting for transfers between devices: 106 us -> none  [body(): lax.all_to_all(outgoing, ('seq', 'tensor'), split_axis=0, concat_axis=0,...]
    dot_general x20 -> x0, matrix products: 82.7 us -> none  [the longest x8 30 us: one_step(): jnp.einsum('hqk,khd->hqd', weights.astype(jnp.bfloat16), value_block, pre...]
    gather x9 -> x0, local copies, waits for them, and re-layouts: 55.4 us -> none  [the longest x8 49.2 us: one_step(): doc_ids[key_pos][None, :] == query_docs[:, None]]
    reduce_scatter x1 -> x0, waiting for transfers between devices: 37.2 us -> none  [body(): lax.psum_scatter(jnp.dot(context, out_weight, preferred_element_type=jnp....]
    reduce_sum x11 -> x1, other arithmetic: 25.8 us -> 1 us  [body(): jnp.sum((doc_ids[None, :] < jnp.arange(1, 4, dtype=jnp.int32)[:, None]).a...]
    slice x13 -> x0, local copies, waits for them, and re-layouts: 17.3 us -> none  [the longest x8 10.2 us: one_step(): block_kv[:, head_width:].reshape(block_rows, heads_dev, HEAD_DIM)]
  transfers between devices with their start and end apart: 4 -> 0, of which waited for: 4 -> 0; matrix products, arithmetic and copies ran while one was open for 2% -> 0% of each run, Pallas kernels for 0% -> 0%
where the time goes in v1:
time: 153 us; the launch traced here: 150 us
  Pallas kernels  144 us (94%)
  local copies, waits for them, and re-layouts  4.46 us (3%)
  other arithmetic  1.67 us (1%)
    pallas_call x1, Pallas kernels, feed_forward(): pl.pallas_call(ff_kernel, name='feed_forward', out_shape=[jax.ShapeDtypeS...  48.4 us
    pallas_call x1, Pallas kernels, project(): pl.pallas_call(qkv_kernel, name='project', out_shape=[jax.ShapeDtypeStruc...  44.3 us
    pallas_call x1, Pallas kernels, merge(): pl.pallas_call(out_kernel, name='merge', out_shape=like(stream), in_specs...  31.9 us
    pallas_call x1, Pallas kernels, attend(): pl.pallas_call(functools.partial(attention_kernel, chunks=tiles // 2, til...  19.6 us

profile of v1, /device:TPU:0, one launch (start us, length us, event | category | flops | bytes accessed | tf_op | source)
XLA Modules:
  0.0 150.4 jit_solution(15614908034435030514)
XLA Ops:
  0.0 1.0 convert_reduce_fusion
  1.0 0.7 pad_add_fusion.info_ref
  1.7 1.3 reshape.23.gain_ref
  3.0 1.3 reshape.24.gain_ref
  4.2 48.4 %feed_forward.1 = (bf16[8,16,2048]{2,1,0:T(8,128)(2,1)}, bf16[2048,256]{1,0:T(8,128)(2,1)}, bf16[2048,256]{1,0:T(8,128)(2,1)}, bf16[2048,256]{1,0:T(8,128)(2,1)}, bf16[256,2048]{1,0:T(8,128)(2,1)}) custom-call(bf16[1024,2048]{1,0:T(8,128)(2,1)} %tok_hbm.1, bf16[1,2048]{1,0:T(2,128)(2,1)} %reshape.23.gain_ref, bf16[2048,1024]{1,0:T(8,128)(2,1)} %wg_hbm.1, ...), custom_call_target="tpu_custom_call" | custom-call | tf_op jit(solution)/shard_map/feed_forward/pallas_call | solution.py:759
  52.7 44.3 %project.1 = (bf16[16,2,2,2,16,128]{5,4,3,2,1,0:T(8,128)(2,1)}, bf16[16,8,2,2,16,256]{5,4,3,2,1,0:T(8,128)(2,1)}) custom-call(bf16[8,16,2048]{2,1,0:T(8,128)(2,1)} %get-tuple-element.12.stream_ref, bf16[1,2048]{1,0:T(2,128)(2,1)} %reshape.24.gain_ref, bf16[2048,256]{1,0:T(8,128)(2,1)} %q_hbm.3, bf16[2048,256]{1,0:T(8,128)(2,1)} %k_hbm.3, ...), custom_call_target="tpu_custom_call" | custom-call | tf_op jit(solution)/shard_map/project/pallas_call | solution.py:790
  97.0 19.6 %attend.1 = bf16[16,128,128]{2,1,0:T(8,128)(2,1)} custom-call(s32[4]{0:T(128)} %pad_add_fusion.info_ref, bf16[16,128,128]{2,1,0:T(8,128)(2,1)} %bitcast.8, bf16[16,512,256]{2,1,0:T(8,128)(2,1)} %bitcast.5), custom_call_target="tpu_custom_call" | custom-call | tf_op jit(solution)/shard_map/attend/pallas_call | solution.py:817
  116.6 31.9 %merge.1 = bf16[8,16,2048]{2,1,0:T(8,128)(2,1)} custom-call(bf16[16,2,2,2,16,128]{5,4,3,2,1,0:T(8,128)(2,1)} %bitcast.7, bf16[8,16,2048]{2,1,0:T(8,128)(2,1)} %get-tuple-element.12.stream_ref, bf16[256,2048]{1,0:T(8,128)(2,1)} %o_hbm.3, bf16[256,2048]{1,0:T(8,128)(2,1)} %get-tuple-element.18.so_hbm), custom_call_target="tpu_custom_call" | custom-call | tf_op jit(solution)/shard_map/merge/pallas_call | solution.py:829
  148.6 1.9 %copy.14 = bf16[128,2048]{1,0:T(8,128)(2,1)} copy(bf16[128,2048]{1,0:T(8,128)(2,1)} %bitcast.6) | data formatting | bytes 1048576
  (1 shorter events, 0.0 us)

commit v2 on v1

v2 whole, which is shorter than its diff:
```python
import functools

import jax
import jax.numpy as jnp
import numpy as np
from jax import lax
from jax.experimental import pallas as pl
from jax.experimental.pallas import tpu as pltpu
from jax.sharding import PartitionSpec as P

HEAD_DIM = 128
EPSILON = 1e-05
ROPE_BASE = 500000.0
NEGATIVE = -1e30
MESH = pl.DeviceIdType.MESH
F32 = jnp.float32
BF16 = jnp.bfloat16
VMEM_LIMIT = 60 * 1024 * 1024


def place():
    s = lax.axis_index("seq")
    c = lax.axis_index("tensor")
    return s, c, s // 4, s % 4, c // 2, c % 2


def remote(src, dst, send_sem, recv_sem, seq, tensor):
    return pltpu.make_async_remote_copy(
        src_ref=src,
        dst_ref=dst,
        send_sem=send_sem,
        recv_sem=recv_sem,
        device_id={"dp": lax.axis_index("dp"), "seq": seq, "tensor": tensor},
        device_id_type=MESH,
    )


def arrived(dst, recv_sem):
    pltpu.make_async_copy(dst, dst, recv_sem).wait()


def greet_signal(partners):
    barrier = pltpu.get_barrier_semaphore()
    for seq, tensor in partners:
        pl.semaphore_signal(
            barrier,
            inc=1,
            device_id={"dp": lax.axis_index("dp"), "seq": seq, "tensor": tensor},
            device_id_type=MESH,
        )


def greet_wait(partners):
    pl.semaphore_wait(pltpu.get_barrier_semaphore(), len(partners))


def greet(partners):
    greet_signal(partners)
    greet_wait(partners)


def normalized(values, gain):
    mean_square = jnp.mean(values * values, axis=-1, keepdims=True)
    gain = gain.reshape((1,) * (values.ndim - 1) + gain.shape)
    return (values * lax.rsqrt(mean_square + EPSILON) * gain).astype(BF16)


class RingSum:
    def __init__(self, send, recv, send_sem, recv_sem, s, z, k):
        self.send, self.recv = send, recv
        self.send_sem, self.recv_sem = send_sem, recv_sem
        self.s, self.z = s, z
        self.up = (z + 1) % 4
        self.down = (z + 3) % 4
        self.far = (z + 2) % 4
        self.up_c = self.up * 2 + k
        self.down_c = self.down * 2 + k

    def copies(self, ch, phase):
        part = pl.ds(0, 2) if phase == 0 else pl.ds(2, 1)
        made = []
        for d, target in ((0, self.up_c), (1, self.down_c)):
            made.append(
                remote(
                    self.send.at[ch, d, part],
                    self.recv.at[ch, d, part],
                    self.send_sem.at[ch, d, phase],
                    self.recv_sem.at[ch, d, phase],
                    self.s,
                    target,
                )
            )
        return made

    def first(self, ch, value):
        self.send[ch, 0, 0] = value(self.far, 0).astype(BF16)
        self.send[ch, 0, 1] = value(self.up, 1).astype(BF16)
        self.send[ch, 1, 0] = value(self.far, 1).astype(BF16)
        self.send[ch, 1, 1] = value(self.down, 0).astype(BF16)
        for copy in self.copies(ch, 0):
            copy.start()

    def second(self, ch, value):
        for copy in self.copies(ch, 0):
            copy.wait_recv()
        self.send[ch, 0, 2] = (value(self.up, 0) + self.recv[ch, 0, 0].astype(F32)).astype(BF16)
        self.send[ch, 1, 2] = (value(self.down, 1) + self.recv[ch, 1, 0].astype(F32)).astype(BF16)
        for copy in self.copies(ch, 1):
            copy.start()

    def third(self, ch, value):
        for copy in self.copies(ch, 1):
            copy.wait_recv()
        one = (
            value(self.z, 0)
            + self.recv[ch, 0, 2].astype(F32)
            + self.recv[ch, 1, 1].astype(F32)
        )
        two = (
            value(self.z, 1)
            + self.recv[ch, 0, 1].astype(F32)
            + self.recv[ch, 1, 2].astype(F32)
        )
        return one, two

    def finish(self, ch):
        for phase in range(2):
            for copy in self.copies(ch, phase):
                copy.wait_send()


def rope_table(groups, base_rows):
    half = HEAD_DIM // 2
    frequency = ROPE_BASE ** (-(np.arange(half, dtype=np.float64) / half))
    angles = np.arange(groups * base_rows, dtype=np.float64)[:, None] * frequency[None, :]
    cosine, sine = np.cos(angles), np.sin(angles)
    table = np.concatenate([cosine, cosine, -sine, sine], axis=1).astype(np.float32)
    return table.reshape(groups, 16, 2, 2, 16, 4 * half)


ORDER = (
    "H0", "G0", "D0", "H1", "A0", "D1", "W1", "H2", "A1", "D2", "W2", "H3", "B0", "A2", "D3", "B1",
    "C0", "A3", "W3", "B2", "C1", "N0", "B3", "C2", "N1", "C3", "R0", "N2", "W4", "R1", "N3", "Q0",
    "R2", "Q1", "F0", "Q2", "R3", "F1", "Q3", "W5", "E0", "F2", "E1", "F3", "E2", "E3",
)


GATHERS = 15


def front_kernel(
    tok_hbm, mlp_gain_ref, wg_hbm, wu_hbm, wd_hbm, attn_gain_ref, q_hbm, k_hbm, v_hbm, o_hbm, table_hbm,
    stream_ref, q_out, kv_out, wo_out,
    tok, wg, wu, wd, xn, hid, mine, csend, crecv, zsend, zrecv, sstage, xg, w, tab, qst, kvst,
    tok_sem, gu_sem, wd_sem, wsem_s, wsem_r, csem_s, csem_r, zsem_s, zsem_r, ssem_s, ssem_r,
    w_sem, tab_sem, own_s, own_r, relay_s, relay_r, q_s, q_r, kv_s, kv_r, yf_s, yf_r,
    f1_s, f1_r, f2_s, f2_r, g_s, g_r,
):
    s, c, y, x, z, k = place()
    sib = c + 1 - 2 * k
    ff = wg.shape[1]
    width = tok.shape[1]
    gu_tiles = 4
    gu_cols = ff // gu_tiles
    up, down, far = (z + 1) % 4, (z + 3) % 4, (z + 2) % 4
    up_c, down_c = up * 2 + k, down * 2 + k
    other_s = (1 - y) * 4 + x
    core_of_rows = x // 2

    def pair_of(ch):
        return (s // 2 + 1 + ch) % 4

    def source_of(ch, pair):
        return (pair + 3 - ch) % 4

    def tok_copies(ch):
        a = pair_of(ch) * 2
        low = pl.ds(pl.multiple_of(a * 64, 128), 128)
        high = pl.ds(pl.multiple_of((14 - a) * 64, 128), 128)
        return [
            pltpu.make_async_copy(tok_hbm.at[low], tok.at[low], tok_sem.at[ch, 0]),
            pltpu.make_async_copy(tok_hbm.at[high], tok.at[high], tok_sem.at[ch, 1]),
        ]

    def gu_copies(n):
        cols = pl.ds(n * gu_cols, gu_cols)
        return [
            pltpu.make_async_copy(wg_hbm.at[:, cols], wg.at[:, cols], gu_sem.at[n, 0]),
            pltpu.make_async_copy(wu_hbm.at[:, cols], wu.at[:, cols], gu_sem.at[n, 1]),
        ]

    wd_copy = pltpu.make_async_copy(wd_hbm, wd, wd_sem.at[0])
    own_weights = [
        pltpu.make_async_copy(src, w.at[i], w_sem.at[i]) for i, src in enumerate((q_hbm, k_hbm, v_hbm))
    ]
    table_copies = [
        pltpu.make_async_copy(
            table_hbm.at[:, 15 - s if half else s, :, k], tab.at[:, half], tab_sem.at[half]
        )
        for half in range(2)
    ]
    weight_sends = [
        remote(src, dst, wsem_s.at[i], wsem_r.at[i], s, sib)
        for i, (src, dst) in enumerate(
            ((q_hbm, w.at[3]), (k_hbm, w.at[4]), (v_hbm, w.at[5]))
        )
    ]

    partners = [(s, sib), (s, up_c), (s, down_c)]
    partners += [((s + d) % 8, c) for d in range(1, 8)]
    partners += [(y * 4 + (x + d) % 4, sib) for d in range(1, 4)]
    for copy in tok_copies(0):
        copy.start()
    for n in range(gu_tiles):
        for copy in gu_copies(n):
            copy.start()
    greet_signal(partners)
    wd_copy.start()
    for ch in range(1, 4):
        for copy in tok_copies(ch):
            copy.start()
    for copy in own_weights + table_copies:
        copy.start()

    def token_rows(ch):
        a = pair_of(ch) * 2
        low = tok[pl.ds(pl.multiple_of(a * 64, 128), 128), :]
        high = tok[pl.ds(pl.multiple_of((14 - a) * 64, 128), 128), :]
        return low, high

    def step_H(ch):
        for copy in tok_copies(ch):
            copy.wait()
        low, high = token_rows(ch)
        gain = mlp_gain_ref[...].astype(F32)
        xn[0:128, :] = normalized(low.astype(F32), gain)
        xn[128:256, :] = normalized(high.astype(F32), gain)
        for n in range(gu_tiles):
            if ch == 0:
                for copy in gu_copies(n):
                    copy.wait()
            cols = slice(n * gu_cols, (n + 1) * gu_cols)
            gate = jnp.dot(xn[...], wg[:, cols], preferred_element_type=F32)
            up_part = jnp.dot(xn[...], wu[:, cols], preferred_element_type=F32)
            hid[:, cols] = (gate / (1.0 + jnp.exp(-gate)) * up_part).astype(BF16)

    def core_copy(ch):
        return remote(csend.at[ch], crecv.at[ch], csem_s.at[ch], csem_r.at[ch], s, sib)

    def step_G(ch):
        greet_wait(partners)
        for copy in weight_sends:
            copy.start()
        gather_own().start()
        for d in range(2):
            gather(d).start()

    def step_D(ch):
        if ch == 0:
            wd_copy.wait()
        cols_n = 256
        for n in range(width // cols_n):
            cols = slice(n * cols_n, (n + 1) * cols_n)
            part = jnp.dot(hid[...], wd[:, cols], preferred_element_type=F32)
            part = part.reshape(4, 2, 2, 16, cols_n)
            even, odd = part[:, :, 0], part[:, :, 1]
            mine[ch, :, :, :, cols] = jnp.where(k == 0, even, odd)
            csend[ch, :, :, :, cols] = jnp.where(k == 0, odd, even).astype(BF16)
        core_copy(ch).start()

    x_up, x_down, x_far = (x + 1) % 4, (x + 3) % 4, (x + 2) % 4
    slice_rows = o_hbm.shape[0] // 8

    def gather_own():
        mine_rows = o_hbm.at[pl.ds(pl.multiple_of(slice_rows * s, slice_rows), slice_rows)]
        return pltpu.make_async_copy(mine_rows, wo_out.at[z, k, y, x], g_r.at[GATHERS])

    def gather(i):
        half = slice_rows // 2
        if i < 2:
            src = o_hbm.at[pl.ds(pl.multiple_of(slice_rows * s, slice_rows), slice_rows)]
            dst, to = wo_out.at[z, k, y, x], (s, up_c if i == 0 else down_c)
        elif i < 4:
            d = i - 2
            dst = wo_out.at[up if d else down, k, y, x, pl.ds(d * half, half)]
            src, to = dst, (s, down_c if d else up_c)
        elif i == 4:
            dst = wo_out.at[:, k, y, x]
            src, to = dst, (other_s, c)
        elif i < 9:
            d = (i - 5) % 2
            dst = wo_out.at[:, k, y if i < 7 else 1 - y, x]
            src, to = dst, (y * 4 + (x_down if d else x_up), c)
        elif i < 11:
            d = i - 9
            dst = wo_out.at[pl.ds(2 * d, 2), k, :, x_up if d else x_down]
            src, to = dst, (y * 4 + (x_down if d else x_up), c)
        else:
            dst = wo_out.at[:, k, :, (x, x_up, x_down, x_far)[i - 11]]
            src, to = dst, (s, sib)
        return remote(src, dst, g_s.at[i], g_r.at[i], *to)

    def gather_wait(i):
        half = slice_rows // 2
        if i < 2:
            dst = wo_out.at[up if i else down, k, y, x]
        elif i < 4:
            dst = wo_out.at[far, k, y, x, pl.ds((i - 2) * half, half)]
        elif i == 4:
            dst = wo_out.at[:, k, 1 - y, x]
        elif i < 9:
            dst = wo_out.at[:, k, y if i < 7 else 1 - y, x_up if (i - 5) % 2 else x_down]
        elif i < 11:
            dst = wo_out.at[pl.ds(2 * (i - 9), 2), k, :, x_far]
        else:
            dst = wo_out.at[:, 1 - k, :, (x, x_up, x_down, x_far)[i - 11]]
        arrived(dst, g_r.at[i])

    def step_W(i):
        waits, starts = (
            ((0, 1), (2, 3)),
            ((2, 3), (4, 5, 6)),
            ((4,), (7, 8, 11)),
            ((5, 6, 7, 8), (9, 10, 12, 13)),
            ((9, 10), (14,)),
        )[i - 1]
        if i == 2:
            gather_own().wait()
        for j in waits:
            gather_wait(j)
        for j in starts:
            gather(j).start()

    ring = RingSum(zsend, zrecv, zsem_s, zsem_r, s, z, k)

    def piece(ch):
        def value(zd, t):
            block = jnp.where(zd < 2, t, 3 - t)
            return mine[ch, block, zd % 2] + crecv[ch, block, zd % 2].astype(F32)

        return value

    def step_A(ch):
        core_copy(ch).wait_recv()
        ring.first(ch, piece(ch))

    def step_B(ch):
        ring.second(ch, piece(ch))

    def seq_copy(ch, t, target):
        return remote(
            sstage.at[ch, t], stream_ref.at[s], ssem_s.at[ch, t], ssem_r.at[s], target, c
        )

    def step_C(ch):
        totals = ring.third(ch, piece(ch))
        a = pair_of(ch) * 2
        for t in range(2):
            block = jnp.where(z < 2, a + t, 15 - a - t)
            start = pl.multiple_of(block * 64 + (2 * (z % 2) + k) * 16, 16)
            rows = tok[pl.ds(start, 16), :].astype(F32)
            result = (totals[t] + rows).astype(BF16)
            if ch < 3:
                sstage[ch, t] = result
                seq_copy(ch, t, a + t).start()
            else:

                @pl.when(s == a + t)
                def _():
                    stream_ref[s] = result

                @pl.when(s != a + t)
                def _():
                    sstage[ch, t] = result
                    seq_copy(ch, t, a + t).start()

    def own_copies(ch):
        return [
            remote(xg.at[ch, :, z], xg.at[ch, :, z], own_s.at[ch, d], own_r.at[ch, d], s, target)
            for d, target in ((0, up_c), (1, down_c))
        ]

    def step_N(ch):
        g = 2 * source_of(ch, s // 2)
        if ch < 3:
            for t in range(2):
                arrived(stream_ref.at[g + t], ssem_r.at[g + t])
        else:
            other = g + 1 - s % 2
            arrived(stream_ref.at[other], ssem_r.at[other])
        gain = attn_gain_ref[...].astype(F32)
        xg[ch, :, z] = normalized(stream_ref[pl.ds(g, 2)].astype(F32), gain)
        for copy in own_copies(ch):
            copy.start()

    def relay_copies(ch):
        return [
            remote(
                xg.at[ch, d, source], xg.at[ch, d, source],
                relay_s.at[ch, d], relay_r.at[ch, d], s, target,
            )
            for d, source, target in ((0, down, up_c), (1, up, down_c))
        ]

    def step_R(ch):
        arrived(xg.at[ch, :, down], own_r.at[ch, 0])
        arrived(xg.at[ch, :, up], own_r.at[ch, 1])
        for copy in relay_copies(ch):
            copy.start()

    def out_rows(ch, sy, sx):
        return pl.ds(4 * source_of(ch, 2 * sy + sx // 2), 4)

    def q_far(ch, d):
        hx = (x + d) % 4
        return remote(
            qst.at[ch, hx], q_out.at[out_rows(ch, y, x), x % 2, :, k],
            q_s.at[ch, d], q_r.at[ch, x % 2, k], y * 4 + hx, z * 2 + core_of_rows,
        )

    def q_near(ch):
        return pltpu.make_async_copy(
            qst.at[ch, x], q_out.at[out_rows(ch, y, x), x % 2, :, k], q_r.at[ch, x % 2, k]
        )

    def kv_send(ch, d):
        hx = (x + d) % 4
        src = kvst.at[ch, hx]
        dst = kv_out.at[out_rows(ch, y, x), s, :, k]
        if d == 0:
            return pltpu.make_async_copy(src, dst, kv_r.at[ch, x])
        return remote(src, dst, kv_s.at[ch, d], kv_r.at[ch, x], y * 4 + hx, c)

    def y_forward(ch, d):
        sx = (x + d) % 4
        part = kv_out.at[out_rows(ch, y, sx), y * 4 + sx, :, k]
        src = kvst.at[ch, x] if d == 0 else part
        return remote(src, part, yf_s.at[ch, d], yf_r.at[ch, sx], other_s, c)

    def core_forwards(ch, which):
        sy = y if which == 0 else 1 - y
        send, recv = (f1_s, f1_r) if which == 0 else (f2_s, f2_r)
        made = []
        for h in range(2):
            part = kv_out.at[out_rows(ch, sy, 2 * h), pl.ds(sy * 4 + 2 * h, 2), :, k]
            made.append(remote(part, part, send.at[ch, h], recv.at[ch, h], s, sib))
        return made

    def rope(values, cosine, sine):
        return values * cosine + pltpu.roll(values, HEAD_DIM // 2, 1) * sine

    def step_Q(ch):
        for d in range(2):
            arrived(xg.at[ch, d, far], relay_r.at[ch, d])
        if ch == 0:
            for copy in own_weights + table_copies:
                copy.wait()
            for i, copy in enumerate(weight_sends):
                copy.wait_recv()
        lhs = xg[ch].reshape(128, width)
        trig = tab[pl.ds(2 * source_of(ch, s // 2), 2)].reshape(128, 2 * HEAD_DIM)
        cosine, sine = trig[:, :HEAD_DIM], trig[:, HEAD_DIM:]
        for part in range(2):
            core = k if part == 0 else 1 - k
            kf = jnp.dot(lhs, w[3 * part + 1], preferred_element_type=F32)
            vf = jnp.dot(lhs, w[3 * part + 2], preferred_element_type=F32)
            qf = jnp.dot(lhs, w[3 * part], preferred_element_type=F32)
            for hh in range(2):
                cols = slice(hh * HEAD_DIM, (hh + 1) * HEAD_DIM)
                hx = 2 * core + hh
                qst[ch, hx] = rope(qf[:, cols], cosine, sine).astype(BF16).reshape(4, 2, 16, HEAD_DIM)
                kvst[ch, hx, :, :, :, :HEAD_DIM] = (
                    rope(kf[:, cols], cosine, sine).astype(BF16).reshape(4, 2, 16, HEAD_DIM)
                )
                kvst[ch, hx, :, :, :, HEAD_DIM:] = vf[:, cols].astype(BF16).reshape(4, 2, 16, HEAD_DIM)
        for d in (2, 1, 3, 0):
            kv_send(ch, d).start()
        y_forward(ch, 0).start()
        for d in (2, 1, 3):
            q_far(ch, d).start()

        @pl.when(core_of_rows == k)
        def _():
            q_near(ch).start()

        @pl.when(core_of_rows != k)
        def _():
            q_far(ch, 0).start()

    def step_F(ch):
        for d in (1, 3, 2, 0):
            sx = (x + d) % 4
            arrived(kv_out.at[out_rows(ch, y, sx), y * 4 + sx, :, k], kv_r.at[ch, sx])
            if d:
                y_forward(ch, d).start()
        for copy in core_forwards(ch, 0):
            copy.start()

    def step_E(ch):
        for sx in range(4):
            arrived(kv_out.at[out_rows(ch, 1 - y, sx), (1 - y) * 4 + sx, :, k], yf_r.at[ch, sx])
        for copy in core_forwards(ch, 1):
            copy.start()

    steps = dict(
        H=step_H, G=step_G, D=step_D, A=step_A, B=step_B, C=step_C, N=step_N, R=step_R, Q=step_Q,
        F=step_F, E=step_E, W=step_W,
    )
    for name in ORDER:
        steps[name[0]](int(name[1]))

    for ch in range(4):
        core_copy(ch).wait_send()
        ring.finish(ch)
        a = pair_of(ch) * 2
        for t in range(2):
            if ch < 3:
                seq_copy(ch, t, a + t).wait_send()
            else:

                @pl.when(s != a + t)
                def _():
                    seq_copy(ch, t, a + t).wait_send()

        for copy in own_copies(ch) + relay_copies(ch):
            copy.wait_send()
        for d in range(4):
            if d:
                kv_send(ch, d).wait_send()
                q_far(ch, d).wait_send()
            y_forward(ch, d).wait_send()

        @pl.when(core_of_rows != k)
        def _():
            q_far(ch, 0).wait_send()

        for which in range(2):
            for copy in core_forwards(ch, which):
                copy.wait_send()
        for aa in range(2):
            sx = 2 * k + aa
            for kk in range(2):
                arrived(q_out.at[out_rows(ch, y, sx), aa, :, kk], q_r.at[ch, aa, kk])
        for h in range(2):
            for sy, recv in ((y, f1_r), (1 - y, f2_r)):
                arrived(
                    kv_out.at[out_rows(ch, sy, 2 * h), pl.ds(sy * 4 + 2 * h, 2), :, 1 - k],
                    recv.at[ch, h],
                )
    for copy in weight_sends:
        copy.wait_send()
    for i in range(GATHERS):
        gather(i).wait_send()
    for i in range(11, GATHERS):
        gather_wait(i)


def attention_kernel(doc_ref, q_ref, kv_ref, out_ref, *, chunks, tile):
    log2e = 1.4426950408889634
    factor = HEAD_DIM ** (-0.5) * log2e
    half_rows = tile // 4
    s, c, y, x, z, k = place()
    first_block = 4 * y + 2 * k
    starts_of = [jnp.sum((doc_ref[...] < d).astype(jnp.int32)) for d in range(1, 4)]

    def row_start(position):
        start = jnp.zeros_like(position)
        for d in range(3):
            start = jnp.where(starts_of[d] <= position, starts_of[d], start)
        return start

    def low_first(g):
        return g * (2 * tile) + first_block * 64

    def high_first(g):
        return g * (2 * tile) + (14 - first_block) * 64

    def low_positions(g):
        row = lax.broadcasted_iota(jnp.int32, (128, 1), 0)
        return low_first(g) + row

    def high_positions(g):
        row = lax.broadcasted_iota(jnp.int32, (128, 1), 0)
        return high_first(g) + jnp.where(row < 64, row + 64, row - 64)

    def key_positions(t):
        col = lax.broadcasted_iota(jnp.int32, (1, tile), 1)
        flipped = (tile // 64 - 1 - col // 64) * 64 + col % 64
        return t * tile + jnp.where(t % 2 == 0, col, flipped)

    def update(state, queries, t, allowed):
        highest, total, weighted = state
        keys = kv_ref[t, :, :HEAD_DIM]
        scores = lax.dot_general(
            queries, keys, (((1,), (1,)), ((), ())), preferred_element_type=F32
        ) * factor
        if allowed is not None:
            scores = jnp.where(allowed, scores, NEGATIVE)
        new_highest = jnp.maximum(highest, jnp.max(scores, axis=1, keepdims=True))
        weights = jnp.exp2(scores - new_highest)
        if allowed is not None:
            weights = jnp.where(allowed, weights, 0.0)
        rescale = jnp.exp2(highest - new_highest)
        total = total * rescale + jnp.sum(weights, axis=1, keepdims=True)
        weighted = weighted * rescale + jnp.dot(
            weights.astype(BF16), kv_ref[t, :, HEAD_DIM:], preferred_element_type=F32
        )
        return new_highest, total, weighted

    def one_chunk(g, carry):
        queries = q_ref[pl.ds(2 * g, 2)].reshape(256, HEAD_DIM)
        positions = jnp.concatenate([low_positions(g), high_positions(g)], axis=0)
        starts = row_start(positions)
        first_tile = row_start(low_first(g)) // tile
        last_start = row_start(high_first(g) + 127)
        plain_tile = jnp.clip((last_start + tile - 1) // tile, first_tile, 2 * g)

        def masked_step(t, state):
            where_keys = key_positions(t)
            allowed = (where_keys <= positions) & (where_keys >= starts)
            return update(state, queries, t, allowed)

        def plain_step(t, state):
            return update(state, queries, t, None)

        state = (
            jnp.full((256, 1), NEGATIVE, F32),
            jnp.zeros((256, 1), F32),
            jnp.zeros((256, HEAD_DIM), F32),
        )
        state = lax.fori_loop(first_tile, plain_tile, masked_step, state)
        state = lax.fori_loop(plain_tile, 2 * g, plain_step, state)
        highest, total, weighted = masked_step(2 * g, state)
        out_ref[2 * g] = (weighted[:128] / total[:128]).astype(BF16)
        t = 2 * g + 1
        where_keys = key_positions(t)
        allowed = (where_keys <= positions[128:]) & (where_keys >= starts[128:])
        highest, total, weighted = update(
            (highest[128:], total[128:], weighted[128:]), queries[128:], t, allowed
        )
        out_ref[t] = (weighted / total).astype(BF16)
        return carry

    lax.fori_loop(0, chunks, one_chunk, 0)


def out_kernel(ctx_ref, stream_ref, wo_hbm, out_ref, cbuf, w, w_sem, x_s, x_r):
    s, c, y, x, z, k = place()
    width = w.shape[1]
    weight_copy = pltpu.make_async_copy(wo_hbm, w, w_sem.at[0])
    weight_copy.start()
    here = x // 2 == k
    barrier = pltpu.get_barrier_semaphore()
    for sx in range(4):
        for sz in range(4):
            seq, tensor = y * 4 + sx, sz * 2 + x // 2

            @pl.when(jnp.logical_not((seq == s) & (tensor == c)))
            def _():
                pl.semaphore_signal(
                    barrier,
                    inc=1,
                    device_id={"dp": lax.axis_index("dp"), "seq": seq, "tensor": tensor},
                    device_id_type=MESH,
                )

    @pl.when(here)
    def _():
        pl.semaphore_wait(barrier, 15)

    @pl.when(jnp.logical_not(here))
    def _():
        pl.semaphore_wait(barrier, 16)

    head = 4 * z + x

    def send(dx, dz, dk):
        aa, tz, tk = (x + dx) % 2, (z + dz) % 4, (k + dk) % 2
        src = ctx_ref.at[:, tz // 2, aa, tz % 2, tk]
        target = y * 4 + 2 * k + aa, tz * 2 + tk
        return src, target

    def far_send(dx, dz, dk):
        src, target = send(dx, dz, dk)
        return remote(src, cbuf.at[head], x_s.at[dx, dz, dk], x_r.at[head], *target)

    def near_send():
        src, _ = send(0, 0, 0)
        return pltpu.make_async_copy(src, cbuf.at[head], x_r.at[head])

    others = [(dx, dz, dk) for dz in (2, 1, 3, 0) for dx in range(2) for dk in range(2)]
    for where in others:
        if where != (0, 0, 0):
            far_send(*where).start()

    @pl.when(here)
    def _():
        near_send().start()

    @pl.when(jnp.logical_not(here))
    def _():
        far_send(0, 0, 0).start()

    weight_copy.wait()
    for h in range(16):
        arrived(cbuf.at[h], x_r.at[h])
    lhs = jnp.concatenate([cbuf[h].reshape(128, HEAD_DIM) for h in range(16)], axis=1)
    cols_n = 256
    for n in range(width // cols_n):
        cols = slice(n * cols_n, (n + 1) * cols_n)
        part = jnp.dot(lhs, w[:, cols], preferred_element_type=F32)
        rows = stream_ref[:, :, cols].astype(F32)
        out_ref[:, :, cols] = (part.reshape(rows.shape) + rows).astype(BF16)

    for where in others:
        if where != (0, 0, 0):
            far_send(*where).wait_send()

    @pl.when(jnp.logical_not(here))
    def _():
        far_send(0, 0, 0).wait_send()


ANY = pl.BlockSpec(memory_space=pl.ANY)
VM = pl.BlockSpec(memory_space=pltpu.VMEM)
SM = pl.BlockSpec(memory_space=pltpu.SMEM)
DMA = pltpu.SemaphoreType.DMA


def params(collective_id):
    return pltpu.CompilerParams(
        collective_id=collective_id, has_side_effects=True, vmem_limit_bytes=VMEM_LIMIT
    )


def like(array):
    return jax.ShapeDtypeStruct(array.shape, array.dtype)


def front(tokens, mlp_gain, gate, up, down, attn_gain, query, key, value, out, table):
    rows, width = tokens.shape
    ff = gate.shape[1]
    cols = query.shape[1]
    return pl.pallas_call(
        front_kernel,
        name="front",
        out_shape=[
            jax.ShapeDtypeStruct((8, 16, width), BF16),
            jax.ShapeDtypeStruct((16, 2, 2, 2, 16, HEAD_DIM), BF16),
            jax.ShapeDtypeStruct((16, 8, 2, 2, 16, 2 * HEAD_DIM), BF16),
            jax.ShapeDtypeStruct((4, 2, 2, 4, out.shape[0] // 8, width), BF16),
        ],
        in_specs=[ANY, VM, ANY, ANY, ANY, VM] + [ANY] * 5,
        out_specs=[VM, ANY, ANY, ANY],
        scratch_shapes=[
            pltpu.VMEM((rows, width), BF16),
            pltpu.VMEM((width, ff), BF16),
            pltpu.VMEM((width, ff), BF16),
            pltpu.VMEM((ff, width), BF16),
            pltpu.VMEM((256, width), BF16),
            pltpu.VMEM((256, ff), BF16),
            pltpu.VMEM((4, 4, 2, 16, width), F32),
            pltpu.VMEM((4, 4, 2, 16, width), BF16),
            pltpu.VMEM((4, 4, 2, 16, width), BF16),
            pltpu.VMEM((4, 2, 3, 16, width), BF16),
            pltpu.VMEM((4, 2, 3, 16, width), BF16),
            pltpu.VMEM((4, 2, 16, width), BF16),
            pltpu.VMEM((4, 2, 4, 16, width), BF16),
            pltpu.VMEM((6, width, cols), BF16),
            pltpu.VMEM((8, 2, 2, 16, 2 * HEAD_DIM), F32),
            pltpu.VMEM((4, 4, 4, 2, 16, HEAD_DIM), BF16),
            pltpu.VMEM((4, 4, 4, 2, 16, 2 * HEAD_DIM), BF16),
            DMA((4, 2)), DMA((4, 2)), DMA((1,)), DMA((3,)), DMA((3,)), DMA((4,)), DMA((4,)),
            DMA((4, 2, 2)), DMA((4, 2, 2)), DMA((4, 2)), DMA((8,)),
            DMA((3,)), DMA((2,)),
            DMA((4, 2)), DMA((4, 2)), DMA((4, 2)), DMA((4, 2)),
            DMA((4, 4)), DMA((4, 2, 2)), DMA((4, 4)), DMA((4, 4)),
            DMA((4, 4)), DMA((4, 4)), DMA((4, 2)), DMA((4, 2)), DMA((4, 2)), DMA((4, 2)),
            DMA((GATHERS,)), DMA((GATHERS + 1,)),
        ],
        compiler_params=params(1),
    )(tokens, mlp_gain, gate, up, down, attn_gain, query, key, value, out, table)


def attend(docs, queries, keys_values):
    tiles = keys_values.shape[0]
    tile = keys_values.shape[1]
    return pl.pallas_call(
        functools.partial(attention_kernel, chunks=tiles // 2, tile=tile),
        name="attend",
        out_shape=like(queries),
        in_specs=[VM, VM, VM],
        out_specs=VM,
        compiler_params=pltpu.CompilerParams(vmem_limit_bytes=VMEM_LIMIT),
    )(docs.reshape(-1, 128), queries, keys_values)


def merge(context, stream, out_weight):
    width = stream.shape[-1]
    return pl.pallas_call(
        out_kernel,
        name="merge",
        out_shape=like(stream),
        in_specs=[ANY, VM, ANY],
        out_specs=VM,
        scratch_shapes=[
            pltpu.VMEM((16, 8, 16, HEAD_DIM), BF16),
            pltpu.VMEM(out_weight.shape, BF16),
            DMA((1,)), DMA((2, 4, 2)), DMA((16,)),
        ],
        compiler_params=params(3),
    )(context, stream, out_weight)


def body(
    tokens, doc_ids, mlp_gain, gate_weight, up_weight, down_weight,
    attn_gain, query_weight, key_weight, value_weight, out_weight,
):
    table = jnp.asarray(rope_table(8, tokens.shape[0]))
    stream, queries, keys_values, whole_out = front(
        tokens, mlp_gain, gate_weight, up_weight, down_weight, attn_gain,
        query_weight, key_weight, value_weight, out_weight, table,
    )
    context = attend(
        doc_ids, queries.reshape(16, 128, HEAD_DIM), keys_values.reshape(16, 512, 2 * HEAD_DIM)
    )
    merged = merge(
        context.reshape(8, 2, 2, 2, 2, 16, HEAD_DIM), stream, whole_out.reshape(-1, tokens.shape[1])
    )
    return merged.reshape(128, tokens.shape[1])


def solution(mesh):
    in_specs = (
        P(("dp", "seq"), None),
        P("dp"),
        P(),
        P(None, "tensor"),
        P(None, "tensor"),
        P("tensor", None),
        P(),
        P(None, "tensor"),
        P(None, "tensor"),
        P(None, "tensor"),
        P("tensor", None),
    )
    out_specs = P(("dp", "seq", "tensor"), None)
    return jax.shard_map(body, mesh=mesh, in_specs=in_specs, out_specs=out_specs, check_vma=False)
```

time: 153 us -> 134 us (0.88)
  Pallas kernels: 144 us -> 131 us
  local copies, waits for them, and re-layouts: 4.46 us -> 1.88 us
  other arithmetic: 1.67 us -> 0 us
    pallas_call x1, Pallas kernels: 31.9 us -> 15.5 us  [merge(): pl.pallas_call(out_kernel, name='merge', out_shape=like(stream), in_specs...]
    pallas_call x1, Pallas kernels: 19.6 us -> 22.2 us  [attend(): pl.pallas_call(functools.partial(attention_kernel, chunks=tiles // 2, til...]
    reshape x2 -> x0, local copies, waits for them, and re-layouts: 2.58 us -> none  [the longest x1 1.29 us: feed_forward(): gain.reshape(1, width)]
    pallas_call x2 -> x1, Pallas kernels: 92.8 us -> 93.3 us  [front(): pl.pallas_call(front_kernel, name='front', out_shape=[jax.ShapeDtypeStruc...]
where the time goes in v2:
time: 134 us; the launch traced here: 133 us
  Pallas kernels  131 us (98%)
  local copies, waits for them, and re-layouts  1.88 us (1%)
    pallas_call x1, Pallas kernels, front(): pl.pallas_call(front_kernel, name='front', out_shape=[jax.ShapeDtypeStruc...  93.3 us
    pallas_call x1, Pallas kernels, attend(): pl.pallas_call(functools.partial(attention_kernel, chunks=tiles // 2, til...  22.2 us
    pallas_call x1, Pallas kernels, merge(): pl.pallas_call(out_kernel, name='merge', out_shape=like(stream), in_specs...  15.5 us

profile of v2, /device:TPU:0, one launch (start us, length us, event | category | flops | bytes accessed | tf_op | source)
XLA Modules:
  0.0 132.9 jit_solution(2619611157902944767)
XLA Ops:
  0.0 93.3 %front.1 = (bf16[8,16,2048]{2,1,0:T(8,128)(2,1)}, bf16[16,2,2,2,16,128]{5,4,3,2,1,0:T(8,128)(2,1)}, bf16[16,8,2,2,16,256]{5,4,3,2,1,0:T(8,128)(2,1)}, bf16[4,2,2,4,32,2048]{5,4,3,2,1,0:T(8,128)(2,1)}) custom-call(bf16[1024,2048]{1,0:T(8,128)(2,1)} %tok_hbm.1, bf16[2048]{0:T(1024)(128)(2,1)} %mlp_gain_ref.1, bf16[2048,1024]{1,0:T(8,128)(2,1)} %wg_hbm.1, ...), custom_call_target="tpu_custom_call" | custom-call | tf_op jit(solution)/shard_map/front/pallas_call | solution.py:744
  93.3 22.2 %attend.1 = bf16[16,128,128]{2,1,0:T(8,128)(2,1)} custom-call(s32[64,128]{1,0:T(8,128)} %bitcast.11, bf16[16,128,128]{2,1,0:T(8,128)(2,1)} %bitcast.10, bf16[16,512,256]{2,1,0:T(8,128)(2,1)} %bitcast.7), custom_call_target="tpu_custom_call" | custom-call | tf_op jit(solution)/shard_map/attend/pallas_call | solution.py:788
  115.5 15.5 %merge.1 = bf16[8,16,2048]{2,1,0:T(8,128)(2,1)} custom-call(bf16[8,2,2,2,2,16,128]{6,5,4,3,2,1,0:T(8,128)(2,1)} %bitcast.8, bf16[8,16,2048]{2,1,0:T(8,128)(2,1)} %get-tuple-element.11.stream_ref, bf16[2048,2048]{1,0:T(8,128)(2,1)} %bitcast.6), custom_call_target="tpu_custom_call" | custom-call | tf_op jit(solution)/shard_map/merge/pallas_call | solution.py:800
  131.0 1.9 %copy.14 = bf16[128,2048]{1,0:T(8,128)(2,1)} copy(bf16[128,2048]{1,0:T(8,128)(2,1)} %bitcast.9) | data formatting | bytes 1048576

commit v3 on v2

--- a/solution.py
+++ b/solution.py
@@ -139,9 +139,10 @@
 
 
 ORDER = (
-    "H0", "G0", "D0", "H1", "A0", "D1", "W1", "H2", "A1", "D2", "W2", "H3", "B0", "A2", "D3", "B1",
-    "C0", "A3", "W3", "B2", "C1", "N0", "B3", "C2", "N1", "C3", "R0", "N2", "W4", "R1", "N3", "Q0",
-    "R2", "Q1", "F0", "Q2", "R3", "F1", "Q3", "W5", "E0", "F2", "E1", "F3", "E2", "E3",
+    "G0", "H0", "W1", "D0", "W2", "H1", "A0", "D1", "H2", "A1", "D2", "W3",
+    "H3", "B0", "A2", "D3", "B1", "C0", "A3", "B2", "C1", "N0", "B3", "C2",
+    "N1", "C3", "R0", "N2", "R1", "N3", "Q0", "W4", "R2", "Q1", "F0", "Q2",
+    "R3", "F1", "Q3", "E0", "F2", "E1", "F3", "E2", "W5", "E3",
 )
 
 
@@ -558,7 +559,6 @@
 def attention_kernel(doc_ref, q_ref, kv_ref, out_ref, *, chunks, tile):
     log2e = 1.4426950408889634
     factor = HEAD_DIM ** (-0.5) * log2e
-    half_rows = tile // 4
     s, c, y, x, z, k = place()
     first_block = 4 * y + 2 * k
     starts_of = [jnp.sum((doc_ref[...] < d).astype(jnp.int32)) for d in range(1, 4)]
@@ -588,23 +588,33 @@
         flipped = (tile // 64 - 1 - col // 64) * 64 + col % 64
         return t * tile + jnp.where(t % 2 == 0, col, flipped)
 
-    def update(state, queries, t, allowed):
+    def scored(queries, t, allowed):
+        scores = lax.dot_general(
+            queries, kv_ref[t, :, :HEAD_DIM], (((1,), (1,)), ((), ())), preferred_element_type=F32
+        ) * factor
+        return scores if allowed is None else jnp.where(allowed, scores, NEGATIVE)
+
+    def top(scores):
+        return jnp.max(scores, axis=1, keepdims=True)
+
+    def lanes(weights):
+        return sum(weights[:, i * 128 : (i + 1) * 128] for i in range(tile // 128))
+
+    def mixed(weights, t):
+        return jnp.dot(weights.astype(BF16), kv_ref[t, :, HEAD_DIM:], preferred_element_type=F32)
+
+    def update(state, queries, tiles, allowed):
         highest, total, weighted = state
-        keys = kv_ref[t, :, :HEAD_DIM]
-        scores = lax.dot_general(
-            queries, keys, (((1,), (1,)), ((), ())), preferred_element_type=F32
-        ) * factor
-        if allowed is not None:
-            scores = jnp.where(allowed, scores, NEGATIVE)
-        new_highest = jnp.maximum(highest, jnp.max(scores, axis=1, keepdims=True))
-        weights = jnp.exp2(scores - new_highest)
-        if allowed is not None:
-            weights = jnp.where(allowed, weights, 0.0)
+        scores = [scored(queries, t, allowed and allowed[i]) for i, t in enumerate(tiles)]
+        new_highest = highest
+        for part in scores:
+            new_highest = jnp.maximum(new_highest, top(part))
         rescale = jnp.exp2(highest - new_highest)
-        total = total * rescale + jnp.sum(weights, axis=1, keepdims=True)
-        weighted = weighted * rescale + jnp.dot(
-            weights.astype(BF16), kv_ref[t, :, HEAD_DIM:], preferred_element_type=F32
-        )
+        total, weighted = total * rescale, weighted * rescale
+        for part, t in zip(scores, tiles):
+            weights = jnp.exp2(part - new_highest)
+            total = total + lanes(weights)
+            weighted = weighted + mixed(weights, t)
         return new_highest, total, weighted
 
     def one_chunk(g, carry):
@@ -614,34 +624,38 @@
         first_tile = row_start(low_first(g)) // tile
         last_start = row_start(high_first(g) + 127)
         plain_tile = jnp.clip((last_start + tile - 1) // tile, first_tile, 2 * g)
+        plain_tile = plain_tile + plain_tile % 2
+
+        t = 2 * g
+        where_keys = key_positions(t)
+        near = scored(queries, t, (where_keys <= positions) & (where_keys >= starts))
+        where_keys = key_positions(t + 1)
+        allowed = (where_keys <= positions[128:]) & (where_keys >= starts[128:])
+        last = scored(queries[128:], t + 1, allowed)
+        highest = top(near)
+        high = jnp.maximum(highest[128:], top(last))
+        highest = jnp.concatenate([highest[:128], high], axis=0)
+        near = jnp.exp2(near - highest)
+        last = jnp.exp2(last - high)
+        total, weighted = lanes(near), mixed(near, t)
+        total = jnp.concatenate([total[:128], total[128:] + lanes(last)], axis=0)
+        weighted = jnp.concatenate([weighted[:128], weighted[128:] + mixed(last, t + 1)], axis=0)
+        state = highest, total, weighted
 
         def masked_step(t, state):
-            where_keys = key_positions(t)
-            allowed = (where_keys <= positions) & (where_keys >= starts)
-            return update(state, queries, t, allowed)
-
-        def plain_step(t, state):
-            return update(state, queries, t, None)
-
-        state = (
-            jnp.full((256, 1), NEGATIVE, F32),
-            jnp.zeros((256, 1), F32),
-            jnp.zeros((256, HEAD_DIM), F32),
-        )
-        state = lax.fori_loop(first_tile, plain_tile, masked_step, state)
-        state = lax.fori_loop(plain_tile, 2 * g, plain_step, state)
-        highest, total, weighted = masked_step(2 * g, state)
-        out_ref[2 * g] = (weighted[:128] / total[:128]).astype(BF16)
-        t = 2 * g + 1
-        where_keys = key_positions(t)
-        allowed = (where_keys <= positions[128:]) & (where_keys >= starts[128:])
-        highest, total, weighted = update(
-            (highest[128:], total[128:], weighted[128:]), queries[128:], t, allowed
-        )
-        out_ref[t] = (weighted / total).astype(BF16)
+            pair = (2 * t, 2 * t + 1)
+            return update(state, queries, pair, [key_positions(i) >= starts for i in pair])
+
+        def plain_step(i, state):
+            return update(state, queries, (2 * i, 2 * i + 1), None)
+
+        state = lax.fori_loop(first_tile // 2, plain_tile // 2, masked_step, state)
+        highest, total, weighted = lax.fori_loop(plain_tile // 2, g, plain_step, state)
+        result = weighted / jnp.sum(total, axis=1, keepdims=True)
+        out_ref[pl.ds(2 * g, 2)] = result.astype(BF16).reshape(2, 128, HEAD_DIM)
         return carry
 
-    lax.fori_loop(0, chunks, one_chunk, 0)
+    lax.fori_loop(0, chunks, one_chunk, 0, unroll=2)
 
 
 def out_kernel(ctx_ref, stream_ref, wo_hbm, out_ref, cbuf, w, w_sem, x_s, x_r):

time: 134 us -> 131 us (0.978)
  Pallas kernels: 131 us -> 128 us
    pallas_call x1, Pallas kernels: 93.3 us -> 91.4 us  [front(): pl.pallas_call(front_kernel, name='front', out_shape=[jax.ShapeDtypeStruc...]
where the time goes in v3:
time: 131 us; the launch traced here: 130 us
  Pallas kernels  128 us (98%)
  local copies, waits for them, and re-layouts  1.88 us (1%)
    pallas_call x1, Pallas kernels, front(): pl.pallas_call(front_kernel, name='front', out_shape=[jax.ShapeDtypeStruc...  91.4 us
    pallas_call x1, Pallas kernels, attend(): pl.pallas_call(functools.partial(attention_kernel, chunks=tiles // 2, til...  21.4 us
    pallas_call x1, Pallas kernels, merge(): pl.pallas_call(out_kernel, name='merge', out_shape=like(stream), in_specs...  15.1 us

profile of v3, /device:TPU:0, one launch (start us, length us, event | category | flops | bytes accessed | tf_op | source)
XLA Modules:
  0.0 129.8 jit_solution(9231839322447982732)
XLA Ops:
  0.0 91.4 %front.1 = (bf16[8,16,2048]{2,1,0:T(8,128)(2,1)}, bf16[16,2,2,2,16,128]{5,4,3,2,1,0:T(8,128)(2,1)}, bf16[16,8,2,2,16,256]{5,4,3,2,1,0:T(8,128)(2,1)}, bf16[4,2,2,4,32,2048]{5,4,3,2,1,0:T(8,128)(2,1)}) custom-call(bf16[1024,2048]{1,0:T(8,128)(2,1)} %tok_hbm.1, bf16[2048]{0:T(1024)(128)(2,1)} %mlp_gain_ref.1, bf16[2048,1024]{1,0:T(8,128)(2,1)} %wg_hbm.1, ...), custom_call_target="tpu_custom_call" | custom-call | tf_op jit(solution)/shard_map/front/pallas_call | solution.py:758
  91.4 21.4 %attend.1 = bf16[16,128,128]{2,1,0:T(8,128)(2,1)} custom-call(s32[64,128]{1,0:T(8,128)} %bitcast.11, bf16[16,128,128]{2,1,0:T(8,128)(2,1)} %bitcast.10, bf16[16,512,256]{2,1,0:T(8,128)(2,1)} %bitcast.7), custom_call_target="tpu_custom_call" | custom-call | tf_op jit(solution)/shard_map/attend/pallas_call | solution.py:802
  112.8 15.1 %merge.1 = bf16[8,16,2048]{2,1,0:T(8,128)(2,1)} custom-call(bf16[8,2,2,2,2,16,128]{6,5,4,3,2,1,0:T(8,128)(2,1)} %bitcast.8, bf16[8,16,2048]{2,1,0:T(8,128)(2,1)} %get-tuple-element.11.stream_ref, bf16[2048,2048]{1,0:T(8,128)(2,1)} %bitcast.6), custom_call_target="tpu_custom_call" | custom-call | tf_op jit(solution)/shard_map/merge/pallas_call | solution.py:814
  127.9 1.9 %copy.14 = bf16[128,2048]{1,0:T(8,128)(2,1)} copy(bf16[128,2048]{1,0:T(8,128)(2,1)} %bitcast.9) | data formatting | bytes 1048576

commit v4 on v3

--- a/solution.py
+++ b/solution.py
@@ -216,12 +216,14 @@
         for copy in gu_copies(n):
             copy.start()
     greet_signal(partners)
-    wd_copy.start()
-    for ch in range(1, 4):
-        for copy in tok_copies(ch):
+
+    def late_loads():
+        wd_copy.start()
+        for ch in range(1, 4):
+            for copy in tok_copies(ch):
+                copy.start()
+        for copy in own_weights + table_copies:
             copy.start()
-    for copy in own_weights + table_copies:
-        copy.start()
 
     def token_rows(ch):
         a = pair_of(ch) * 2
@@ -240,6 +242,8 @@
             if ch == 0:
                 for copy in gu_copies(n):
                     copy.wait()
+                if n == 1:
+                    late_loads()
             cols = slice(n * gu_cols, (n + 1) * gu_cols)
             gate = jnp.dot(xn[...], wg[:, cols], preferred_element_type=F32)
             up_part = jnp.dot(xn[...], wu[:, cols], preferred_element_type=F32)

time: 131 us -> 131 us (level)
  no operation moved by 1% of the time
where the time goes in v4:
time: 131 us; the launch traced here: 130 us
  Pallas kernels  128 us (98%)
  local copies, waits for them, and re-layouts  1.88 us (1%)
    pallas_call x1, Pallas kernels, front(): pl.pallas_call(front_kernel, name='front', out_shape=[jax.ShapeDtypeStruc...  91.4 us
    pallas_call x1, Pallas kernels, attend(): pl.pallas_call(functools.partial(attention_kernel, chunks=tiles // 2, til...  21.4 us
    pallas_call x1, Pallas kernels, merge(): pl.pallas_call(out_kernel, name='merge', out_shape=like(stream), in_specs...  15.1 us

profile of v4, /device:TPU:0, one launch (start us, length us, event | category | flops | bytes accessed | tf_op | source)
XLA Modules:
  0.0 129.8 jit_solution(16219553775009216142)
XLA Ops:
  0.0 91.4 %front.1 = (bf16[8,16,2048]{2,1,0:T(8,128)(2,1)}, bf16[16,2,2,2,16,128]{5,4,3,2,1,0:T(8,128)(2,1)}, bf16[16,8,2,2,16,256]{5,4,3,2,1,0:T(8,128)(2,1)}, bf16[4,2,2,4,32,2048]{5,4,3,2,1,0:T(8,128)(2,1)}) custom-call(bf16[1024,2048]{1,0:T(8,128)(2,1)} %tok_hbm.1, bf16[2048]{0:T(1024)(128)(2,1)} %mlp_gain_ref.1, bf16[2048,1024]{1,0:T(8,128)(2,1)} %wg_hbm.1, ...), custom_call_target="tpu_custom_call" | custom-call | tf_op jit(solution)/shard_map/front/pallas_call | solution.py:762
  91.4 21.4 %attend.1 = bf16[16,128,128]{2,1,0:T(8,128)(2,1)} custom-call(s32[64,128]{1,0:T(8,128)} %bitcast.11, bf16[16,128,128]{2,1,0:T(8,128)(2,1)} %bitcast.10, bf16[16,512,256]{2,1,0:T(8,128)(2,1)} %bitcast.7), custom_call_target="tpu_custom_call" | custom-call | tf_op jit(solution)/shard_map/attend/pallas_call | solution.py:806
  112.8 15.1 %merge.1 = bf16[8,16,2048]{2,1,0:T(8,128)(2,1)} custom-call(bf16[8,2,2,2,2,16,128]{6,5,4,3,2,1,0:T(8,128)(2,1)} %bitcast.8, bf16[8,16,2048]{2,1,0:T(8,128)(2,1)} %get-tuple-element.11.stream_ref, bf16[2048,2048]{1,0:T(8,128)(2,1)} %bitcast.6), custom_call_target="tpu_custom_call" | custom-call | tf_op jit(solution)/shard_map/merge/pallas_call | solution.py:818
  127.9 1.9 %copy.14 = bf16[128,2048]{1,0:T(8,128)(2,1)} copy(bf16[128,2048]{1,0:T(8,128)(2,1)} %bitcast.9) | data formatting | bytes 1048576
